TPU v7x, 128 devices: a whole 4x4x4 slice. The times are simulated.
128 devices in a mesh: shard: 4 (over x), ctx: 4 (over y_hi, core), tp: 8 (over y_lo, z).
Axes of the slice: x: 4, y: 4 (y_hi: 2, y_lo: 2; y = y_hi * 2 + y_lo), z: 4, core: 2. Of those that a mesh axis runs over, the one named last changes fastest.
Arguments:
- tokens: bfloat16 [12288, 2048], P(('shard', 'ctx')), may hold values from -6 to 6
- cotangent: bfloat16 [12288, 2048], P(('shard', 'ctx')), may hold values from -6 to 6
- lengths: int32 [8], replicated, may hold values from 128 to 3072, as said below
- groups: int32 [8], replicated, may hold values from 0 to 3
- query_weight: float32 [2048, 2048], P(('shard', 'ctx'), 'tp'), may hold values from -0.125 to 0.125
- query_m: float32 [2048, 2048], P(('shard', 'ctx'), 'tp'), may hold values from -64 to 64
- query_v: float32 [2048, 2048], P(('shard', 'ctx'), 'tp'), may hold values from 651.264 to 2580.48
- kv_weight: float32 [2048, 8, 128], P(('shard', 'ctx'), 'tp'), may hold values from -0.125 to 0.125
- kv_m: float32 [2048, 8, 128], P(('shard', 'ctx'), 'tp'), may hold values from -64 to 64
- kv_v: float32 [2048, 8, 128], P(('shard', 'ctx'), 'tp'), may hold values from 651.264 to 2580.48
- out_weight: float32 [2048, 2048], P('tp', ('shard', 'ctx')), may hold values from -4 to 4
- out_m: float32 [2048, 2048], P('tp', ('shard', 'ctx')), may hold values from -4 to 4
- out_v: float32 [2048, 2048], P('tp', ('shard', 'ctx')), may hold values from 0.64 to 2.52
- gate_weight: float32 [2048, 8192], P(('shard', 'ctx'), 'tp'), may hold values from -0.125 to 0.125
- gate_m: float32 [2048, 8192], P(('shard', 'ctx'), 'tp'), may hold values from -20 to 20
- gate_v: float32 [2048, 8192], P(('shard', 'ctx'), 'tp'), may hold values from 58.9824 to 233.472
- up_weight: float32 [2048, 8192], P(('shard', 'ctx'), 'tp'), may hold values from -0.125 to 0.125
- up_m: float32 [2048, 8192], P(('shard', 'ctx'), 'tp'), may hold values from -20 to 20
- up_v: float32 [2048, 8192], P(('shard', 'ctx'), 'tp'), may hold values from 58.9824 to 233.472
- down_weight: float32 [8192, 2048], P('tp', ('shard', 'ctx')), may hold values from -0.0625 to 0.0625
- down_m: float32 [8192, 2048], P('tp', ('shard', 'ctx')), may hold values from -28 to 28
- down_v: float32 [8192, 2048], P('tp', ('shard', 'ctx')), may hold values from 104.448 to 417.792
- norm_gains: float32 [2, 2048], P(None, ('shard', 'ctx')), may hold values from 0.5 to 1.5
- gains_m: float32 [2, 2048], P(None, ('shard', 'ctx')), may hold values from -64 to 64
- gains_v: float32 [2, 2048], P(None, ('shard', 'ctx')), may hold values from 651.264 to 2580.48
Outputs:
- output: bfloat16 [12288, 2048], P(('shard', 'ctx'))
- tokens_grad: bfloat16 [12288, 2048], P(('shard', 'ctx'))
- query_m_new: float32 [2048, 2048], P(('shard', 'ctx'), 'tp')
- query_v_new: float32 [2048, 2048], P(('shard', 'ctx'), 'tp')
- query_new: float32 [2048, 2048], P(('shard', 'ctx'), 'tp')
- kv_m_new: float32 [2048, 8, 128], P(('shard', 'ctx'), 'tp')
- kv_v_new: float32 [2048, 8, 128], P(('shard', 'ctx'), 'tp')
- kv_new: float32 [2048, 8, 128], P(('shard', 'ctx'), 'tp')
- out_m_new: float32 [2048, 2048], P('tp', ('shard', 'ctx'))
- out_v_new: float32 [2048, 2048], P('tp', ('shard', 'ctx'))
- out_new: float32 [2048, 2048], P('tp', ('shard', 'ctx'))
- gate_m_new: float32 [2048, 8192], P(('shard', 'ctx'), 'tp')
- gate_v_new: float32 [2048, 8192], P(('shard', 'ctx'), 'tp')
- gate_new: float32 [2048, 8192], P(('shard', 'ctx'), 'tp')
- up_m_new: float32 [2048, 8192], P(('shard', 'ctx'), 'tp')
- up_v_new: float32 [2048, 8192], P(('shard', 'ctx'), 'tp')
- up_new: float32 [2048, 8192], P(('shard', 'ctx'), 'tp')
- down_m_new: float32 [8192, 2048], P('tp', ('shard', 'ctx'))
- down_v_new: float32 [8192, 2048], P('tp', ('shard', 'ctx'))
- down_new: float32 [8192, 2048], P('tp', ('shard', 'ctx'))
- gains_m_new: float32 [2, 2048], P(None, ('shard', 'ctx'))
- gains_v_new: float32 [2, 2048], P(None, ('shard', 'ctx'))
- gains_new: float32 [2, 2048], P(None, ('shard', 'ctx'))
Inputs may be any that keep to these rules, and one draw needn't show every extreme that they name: Lengths are multiples of 128. Sequence g < 4 belongs to group g; the others belong to any group. The lengths of one group's sequences sum to at most 3072, and to exactly 3072 in some group.
All inputs are finite; a program needn't handle non-finite values.
Results may differ from a plain program's by a relative error of at most 0.013.
The roundings to bfloat16 on the way count: a program that leaves them out, or rounds other values in their place, can miss the bound.
Values may be sent and summed in bfloat16 or wider, within the bound.
No kernel may reach another device: no remote copies, remote signals or barrier semaphores. Data moves between devices by JAX's collectives and lax.ppermute only.
A program may use at most 192 MiB of HBM per device.

v0:
```python
import jax
import jax.numpy as jnp
from jax import lax
from jax.sharding import PartitionSpec as P

D = 2048
HD = 64
FF = 8192
STEP = 5


NORM_EPS = 1e-05
BETA_FIRST = 0.9
BETA_SECOND = 0.95
ADAM_EPS = 1e-08
DECAY_RATE = 0.1
ROPE_BASE = 500000.0
MASKED_SCORE = -1e30


def layout_slots(lengths, groups, group_id, slot_ids):
    seq_count = lengths.shape[0]
    seq_order = jnp.arange(seq_count, dtype=jnp.int32)
    same_group = groups[None, :] == groups[:, None]
    before = seq_order[None, :] < seq_order[:, None]
    starts = jnp.sum(jnp.where(same_group & before, lengths[None, :], 0), axis=1)
    ends = starts + lengths
    inside = (
        (groups == group_id)[:, None]
        & (slot_ids[None, :] >= starts[:, None])
        & (slot_ids[None, :] < ends[:, None])
    )
    document = jnp.sum(jnp.where(inside, seq_order[:, None] + 1, 0), axis=0) - 1
    position = jnp.sum(jnp.where(inside, slot_ids[None, :] - starts[:, None], 0), axis=0)
    document = jnp.where(document < 0, seq_count + slot_ids, document)
    return (document, position)


def rotate(values, position, direction):
    half_dim = values.shape[-1] // 2
    frequency = ROPE_BASE ** (-2.0 * jnp.arange(half_dim, dtype=jnp.float32) / values.shape[-1])
    angles = position.astype(jnp.float32)[:, None] * frequency[None, :]
    cosine = jnp.cos(angles)[:, None, :]
    sine_part = direction * jnp.sin(angles)[:, None, :]
    first_half = values[..., :half_dim]
    second = values[..., half_dim:]
    return jnp.concatenate(
        [first_half * cosine - second * sine_part, second * cosine + first_half * sine_part],
        axis=-1,
    )


def adamw_step(weight, first, second, grad, rate, decay):
    first_new = BETA_FIRST * first + (1.0 - BETA_FIRST) * grad
    second_new = BETA_SECOND * second + (1.0 - BETA_SECOND) * grad * grad
    first_hat = first_new / (1.0 - BETA_FIRST**STEP)
    second_hat = second_new / (1.0 - BETA_SECOND**STEP)
    weight_new = weight - rate * (first_hat / (jnp.sqrt(second_hat) + ADAM_EPS) + decay * weight)
    return (first_new, second_new, weight_new)


def norm_backward(d_normed, pre_scaled, inverse, gain_row):
    grad_gain = jnp.sum(d_normed * pre_scaled, axis=0)
    scaled = d_normed * gain_row
    d_input = inverse * (
        scaled - pre_scaled * jnp.mean(scaled * pre_scaled, axis=-1, keepdims=True)
    )
    return (grad_gain, d_input)


def per_device(
    tokens,
    cotangent,
    lengths,
    groups,
    query_weight,
    query_m,
    query_v,
    kv_weight,
    kv_m,
    kv_v,
    out_weight,
    out_m,
    out_v,
    gate_weight,
    gate_m,
    gate_v,
    up_weight,
    up_m,
    up_v,
    down_weight,
    down_m,
    down_v,
    norm_gains,
    gains_m,
    gains_v,
):
    row_count = tokens.shape[0]
    group_rows = row_count * lax.axis_size("ctx")
    group_id = lax.axis_index("shard")
    ctx_id = lax.axis_index("ctx")
    key_doc, key_pos = layout_slots(
        lengths, groups, group_id, jnp.arange(group_rows, dtype=jnp.int32)
    )
    own_doc, own_pos = layout_slots(
        lengths, groups, group_id, ctx_id * row_count + jnp.arange(row_count, dtype=jnp.int32)
    )
    visible = (own_doc[:, None] == key_doc[None, :]) & (key_pos[None, :] <= own_pos[:, None])
    scale = HD ** (-0.5)
    query_low, key_value_low, out_low, gains_low = (
        lax.all_gather(query_weight.astype(jnp.bfloat16), ("shard", "ctx"), axis=0, tiled=True),
        lax.all_gather(kv_weight.astype(jnp.bfloat16), ("shard", "ctx"), axis=0, tiled=True),
        lax.all_gather(out_weight.astype(jnp.bfloat16), ("shard", "ctx"), axis=1, tiled=True),
        lax.all_gather(norm_gains.astype(jnp.bfloat16), ("shard", "ctx"), axis=1, tiled=True),
    )
    gain_values = gains_low.astype(jnp.float32)
    inputs = tokens.astype(jnp.float32)
    upstream = cotangent.astype(jnp.float32)
    inv_one = lax.rsqrt(jnp.mean(inputs * inputs, axis=-1, keepdims=True) + NORM_EPS)
    pre_one = inputs * inv_one
    normed_one = (pre_one * gain_values[0]).astype(jnp.bfloat16)
    head_count = query_low.shape[1] // HD
    kv_count = key_value_low.shape[1]
    head_share = head_count // kv_count
    query_raw = jnp.dot(normed_one, query_low, preferred_element_type=jnp.float32).reshape(
        row_count, head_count, HD
    )
    queries = rotate(query_raw, own_pos, 1.0).astype(jnp.bfloat16).transpose(1, 0, 2)
    kv_raw = jnp.dot(
        normed_one, key_value_low.reshape(D, kv_count * 2 * HD), preferred_element_type=jnp.float32
    ).reshape(row_count, kv_count, 2 * HD)
    kv_local = jnp.concatenate(
        [rotate(kv_raw[..., :HD], own_pos, 1.0), kv_raw[..., HD:]], axis=-1
    ).astype(jnp.bfloat16)
    kv_whole = lax.all_gather(kv_local, "ctx", axis=0, tiled=True)
    key_heads = jnp.repeat(kv_whole[..., :HD].transpose(1, 0, 2), head_share, axis=0)
    value_heads = jnp.repeat(kv_whole[..., HD:].transpose(1, 0, 2), head_share, axis=0)

    def forward_head(operands):
        query_head, key_head, value_head = operands
        scores = (
            jnp.einsum("rd,kd->rk", query_head, key_head, preferred_element_type=jnp.float32)
            * scale
        )
        scores = jnp.where(visible, scores, MASKED_SCORE)
        row_peak = jnp.max(scores, axis=-1, keepdims=True)
        powers = jnp.exp(scores - row_peak)
        summed = jnp.sum(powers, axis=-1, keepdims=True)
        chances = (powers / summed).astype(jnp.bfloat16)
        mixed_head = jnp.dot(chances, value_head, preferred_element_type=jnp.float32)
        return (mixed_head, (row_peak + jnp.log(summed))[:, 0])

    mixed_heads, log_totals = lax.map(forward_head, (queries, key_heads, value_heads))
    mixed = mixed_heads.transpose(1, 0, 2).reshape(row_count, head_count * HD).astype(jnp.bfloat16)
    attention_term = jnp.dot(mixed, out_low, preferred_element_type=jnp.float32)
    hidden_one = inputs + lax.psum(attention_term, "tp")
    inv_two = lax.rsqrt(jnp.mean(hidden_one * hidden_one, axis=-1, keepdims=True) + NORM_EPS)
    pre_two = hidden_one * inv_two
    normed_two = (pre_two * gain_values[1]).astype(jnp.bfloat16)
    gate_low, up_low, down_low = (
        lax.all_gather(gate_weight.astype(jnp.bfloat16), ("shard", "ctx"), axis=0, tiled=True),
        lax.all_gather(up_weight.astype(jnp.bfloat16), ("shard", "ctx"), axis=0, tiled=True),
        lax.all_gather(down_weight.astype(jnp.bfloat16), ("shard", "ctx"), axis=1, tiled=True),
    )
    gate_value = jnp.dot(normed_two, gate_low, preferred_element_type=jnp.float32)
    up_value = jnp.dot(normed_two, up_low, preferred_element_type=jnp.float32)
    sigmoid_gate = jax.nn.sigmoid(gate_value)
    activated = gate_value * sigmoid_gate
    hidden = (activated * up_value).astype(jnp.bfloat16)
    feedforward_term = jnp.dot(hidden, down_low, preferred_element_type=jnp.float32)
    output = (hidden_one + lax.psum(feedforward_term, "tp")).astype(jnp.bfloat16)
    query_low, key_value_low, out_low, gains_low, gate_low, up_low, down_low = (
        lax.all_gather(query_weight.astype(jnp.bfloat16), ("shard", "ctx"), axis=0, tiled=True),
        lax.all_gather(kv_weight.astype(jnp.bfloat16), ("shard", "ctx"), axis=0, tiled=True),
        lax.all_gather(out_weight.astype(jnp.bfloat16), ("shard", "ctx"), axis=1, tiled=True),
        lax.all_gather(norm_gains.astype(jnp.bfloat16), ("shard", "ctx"), axis=1, tiled=True),
        lax.all_gather(gate_weight.astype(jnp.bfloat16), ("shard", "ctx"), axis=0, tiled=True),
        lax.all_gather(up_weight.astype(jnp.bfloat16), ("shard", "ctx"), axis=0, tiled=True),
        lax.all_gather(down_weight.astype(jnp.bfloat16), ("shard", "ctx"), axis=1, tiled=True),
    )
    gain_values = gains_low.astype(jnp.float32)
    grad_down = jnp.einsum("rf,rd->fd", hidden, cotangent, preferred_element_type=jnp.float32)
    d_hidden = jnp.einsum("rd,fd->rf", cotangent, down_low, preferred_element_type=jnp.float32)
    d_gate = (
        d_hidden * up_value * sigmoid_gate * (1.0 + gate_value * (1.0 - sigmoid_gate))
    ).astype(jnp.bfloat16)
    d_up = (d_hidden * activated).astype(jnp.bfloat16)
    grad_gate = jnp.einsum("rd,rf->df", normed_two, d_gate, preferred_element_type=jnp.float32)
    grad_up = jnp.einsum("rd,rf->df", normed_two, d_up, preferred_element_type=jnp.float32)
    d_two_term = jnp.einsum(
        "rf,df->rd", d_gate, gate_low, preferred_element_type=jnp.float32
    ) + jnp.einsum("rf,df->rd", d_up, up_low, preferred_element_type=jnp.float32)
    d_normed_two = lax.psum(d_two_term, "tp")
    grad_gain_two, d_through_two = norm_backward(d_normed_two, pre_two, inv_two, gain_values[1])
    d_hidden_one = upstream + d_through_two
    d_branch = d_hidden_one.astype(jnp.bfloat16)
    grad_gate_own, grad_up_own, grad_down_own = (
        lax.psum_scatter(grad_gate, ("shard", "ctx"), scatter_dimension=0, tiled=True),
        lax.psum_scatter(grad_up, ("shard", "ctx"), scatter_dimension=0, tiled=True),
        lax.psum_scatter(grad_down, ("shard", "ctx"), scatter_dimension=1, tiled=True),
    )
    grad_out = jnp.einsum("ra,rd->ad", mixed, d_branch, preferred_element_type=jnp.float32)
    d_mixed = jnp.einsum("rd,ad->ra", d_branch, out_low, preferred_element_type=jnp.float32).astype(
        jnp.bfloat16
    )
    d_mixed = d_mixed.reshape(row_count, head_count, HD).transpose(1, 0, 2)

    def backward_head(operands):
        query_head, key_head, value_head, d_head, log_total = operands
        scores = (
            jnp.einsum("rd,kd->rk", query_head, key_head, preferred_element_type=jnp.float32)
            * scale
        )
        scores = jnp.where(visible, scores, MASKED_SCORE)
        chances = jnp.exp(scores - log_total[:, None])
        d_value = jnp.einsum(
            "rk,rd->kd", chances.astype(jnp.bfloat16), d_head, preferred_element_type=jnp.float32
        )
        d_chances = jnp.einsum("rd,kd->rk", d_head, value_head, preferred_element_type=jnp.float32)
        centre = jnp.sum(chances * d_chances, axis=-1, keepdims=True)
        d_scores = (chances * (d_chances - centre)).astype(jnp.bfloat16)
        d_query = jnp.dot(d_scores, key_head, preferred_element_type=jnp.float32) * scale
        d_key = (
            jnp.einsum("rk,rd->kd", d_scores, query_head, preferred_element_type=jnp.float32)
            * scale
        )
        return (d_query, d_key, d_value)

    d_queries, d_keys, d_values = lax.map(
        backward_head, (queries, key_heads, value_heads, d_mixed, log_totals)
    )
    d_keys = d_keys.reshape(kv_count, head_share, group_rows, HD).sum(axis=1).transpose(1, 0, 2)
    d_values = d_values.reshape(kv_count, head_share, group_rows, HD).sum(axis=1).transpose(1, 0, 2)
    d_kv_whole = jnp.concatenate([d_keys, d_values], axis=-1)
    d_kv_own = lax.psum_scatter(d_kv_whole, "ctx", scatter_dimension=0, tiled=True)
    d_kv_low = jnp.concatenate(
        [rotate(d_kv_own[..., :HD], own_pos, -1.0), d_kv_own[..., HD:]], axis=-1
    ).astype(jnp.bfloat16)
    d_kv_low = d_kv_low.reshape(row_count, kv_count * 2 * HD)
    d_query_low = (
        rotate(d_queries.transpose(1, 0, 2), own_pos, -1.0)
        .astype(jnp.bfloat16)
        .reshape(row_count, head_count * HD)
    )
    grad_query = jnp.einsum(
        "rd,ra->da", normed_one, d_query_low, preferred_element_type=jnp.float32
    )
    grad_kv = jnp.einsum(
        "rd,rc->dc", normed_one, d_kv_low, preferred_element_type=jnp.float32
    ).reshape(D, kv_count, 2 * HD)
    d_one_term = jnp.einsum("ra,da->rd", d_query_low, query_low, preferred_element_type=jnp.float32)
    d_one_term = d_one_term + jnp.einsum(
        "rc,dc->rd",
        d_kv_low,
        key_value_low.reshape(D, kv_count * 2 * HD),
        preferred_element_type=jnp.float32,
    )
    d_normed_one = lax.psum(d_one_term, "tp")
    grad_gain_one, d_through_one = norm_backward(d_normed_one, pre_one, inv_one, gain_values[0])
    tokens_grad = (d_hidden_one + d_through_one).astype(jnp.bfloat16)
    grad_gains = jnp.stack([grad_gain_one, grad_gain_two], axis=0)
    grad_query_own, grad_kv_own, grad_out_own, grad_gains_own = (
        lax.psum_scatter(grad_query, ("shard", "ctx"), scatter_dimension=0, tiled=True),
        lax.psum_scatter(grad_kv, ("shard", "ctx"), scatter_dimension=0, tiled=True),
        lax.psum_scatter(grad_out, ("shard", "ctx"), scatter_dimension=1, tiled=True),
        lax.psum_scatter(grad_gains, ("shard", "ctx"), scatter_dimension=1, tiled=True),
    )
    out_fan = max(1, 4 * D // group_rows)
    query_new = adamw_step(query_weight, query_m, query_v, grad_query_own, D ** (-0.5), DECAY_RATE)
    kv_new = adamw_step(kv_weight, kv_m, kv_v, grad_kv_own, D ** (-0.5), DECAY_RATE)
    out_new = adamw_step(out_weight, out_m, out_v, grad_out_own, out_fan ** (-0.5), DECAY_RATE)
    gate_new = adamw_step(gate_weight, gate_m, gate_v, grad_gate_own, D ** (-0.5), DECAY_RATE)
    up_new = adamw_step(up_weight, up_m, up_v, grad_up_own, D ** (-0.5), DECAY_RATE)
    down_new = adamw_step(down_weight, down_m, down_v, grad_down_own, FF ** (-0.5), DECAY_RATE)
    gains_new = adamw_step(norm_gains, gains_m, gains_v, grad_gains_own, 0.5, 0.0)
    return (
        output,
        tokens_grad,
        query_new[0],
        query_new[1],
        query_new[2],
        kv_new[0],
        kv_new[1],
        kv_new[2],
        out_new[0],
        out_new[1],
        out_new[2],
        gate_new[0],
        gate_new[1],
        gate_new[2],
        up_new[0],
        up_new[1],
        up_new[2],
        down_new[0],
        down_new[1],
        down_new[2],
        gains_new[0],
        gains_new[1],
        gains_new[2],
    )


def solution(mesh):
    in_specs = (
        P(("shard", "ctx"), None),
        P(("shard", "ctx"), None),
        P(),
        P(),
        P(("shard", "ctx"), "tp"),
        P(("shard", "ctx"), "tp"),
        P(("shard", "ctx"), "tp"),
        P(("shard", "ctx"), "tp", None),
        P(("shard", "ctx"), "tp", None),
        P(("shard", "ctx"), "tp", None),
        P("tp", ("shard", "ctx")),
        P("tp", ("shard", "ctx")),
        P("tp", ("shard", "ctx")),
        P(("shard", "ctx"), "tp"),
        P(("shard", "ctx"), "tp"),
        P(("shard", "ctx"), "tp"),
        P(("shard", "ctx"), "tp"),
        P(("shard", "ctx"), "tp"),
        P(("shard", "ctx"), "tp"),
        P("tp", ("shard", "ctx")),
        P("tp", ("shard", "ctx")),
        P("tp", ("shard", "ctx")),
        P(None, ("shard", "ctx")),
        P(None, ("shard", "ctx")),
        P(None, ("shard", "ctx")),
    )
    out_specs = (
        P(("shard", "ctx"), None),
        P(("shard", "ctx"), None),
        P(("shard", "ctx"), "tp"),
        P(("shard", "ctx"), "tp"),
        P(("shard", "ctx"), "tp"),
        P(("shard", "ctx"), "tp", None),
        P(("shard", "ctx"), "tp", None),
        P(("shard", "ctx"), "tp", None),
        P("tp", ("shard", "ctx")),
        P("tp", ("shard", "ctx")),
        P("tp", ("shard", "ctx")),
        P(("shard", "ctx"), "tp"),
        P(("shard", "ctx"), "tp"),
        P(("shard", "ctx"), "tp"),
        P(("shard", "ctx"), "tp"),
        P(("shard", "ctx"), "tp"),
        P(("shard", "ctx"), "tp"),
        P("tp", ("shard", "ctx")),
        P("tp", ("shard", "ctx")),
        P("tp", ("shard", "ctx")),
        P(None, ("shard", "ctx")),
        P(None, ("shard", "ctx")),
        P(None, ("shard", "ctx")),
    )
    return jax.shard_map(
        per_device, mesh=mesh, in_specs=in_specs, out_specs=out_specs, check_vma=False
    )
```

profile of v0, /device:TPU:0, one launch (start us, length us, event | category | flops | bytes accessed | tf_op | source)
XLA Modules:
  0.0 1711.6 jit_solution(12078939035604678806)
XLA Ops:
  14.3 24.3 %all_gather.31 = bf16[2,2048]{1,0:T(2,128)(2,1)S(1)} all-gather(bf16[2,128]{1,0:T(2,128)(2,1)S(1)} %convert_element_type.113), channel_id=1, replica_groups=mesh['shard'=4,'ctx'=4,'tp'=8] {'shard','ctx'}, dimensions={1}, use_global_device_ids=true | all-gather | bytes 8704 | tf_op jit(solution)/shard_map/all_gather | solution.py:114
  42.6 20.7 %all_gather.33 = bf16[2048,1,128]{2,0,1:T(8,128)(2,1)S(1)} all-gather(bf16[128,1,128]{2,0,1:T(8,128)(2,1)S(1)} %convert_element_type.118), channel_id=1, replica_groups=mesh['shard'=4,'ctx'=4,'tp'=8] {'shard','ctx'}, dimensions={0}, use_global_device_ids=true | all-gather | bytes 557056 | tf_op jit(solution)/shard_map/all_gather | solution.py:112
  71.6 10.8 all_gather.34
  101.3 57.5 %while.30 = (s32[]{:T(128)}, bf16[4,768,64]{1,2,0:T(8,128)(2,1)S(1)}, f32[4,768]{1,0:T(4,128)}, bf16[4,768,64]{2,1,0:T(8,128)(2,1)}, bf16[4,3072,64]{2,1,0:T(8,1...) while((s32[]{:T(128)}, ...), condition=%wide.region_9.10_spmd.clone.clone, body=%wide.region_6.9_spmd.clone.sunk.clone | while | flops 629931264 | bytes 68099208 | solution.py:153
  169.8 139.9 %all-reduce.5.cloned.1.call-done = f32[768,2048]{1,0:T(8,128)} async-done(((f32[768,2048]{1,0:T(8,128)}), f32[768,2048]{1,0:T(8,128)}) %all-reduce.5.cloned.1.call-update) | async-done | bytes 6291472 | tf_op jit(solution)/shard_map/psum | solution.py:156
  316.7 50.6 %all-gather.10.cloned.1.call-done = bf16[2048,1024]{1,0:T(8,128)(2,1)} async-done(((bf16[128,1024]{1,0:T(8,128)(2,1)}), bf16[2048,1024]{1,0:T(8,128)(2,1)}) %all-gather.10.cloned.1.call-update) | async-done | bytes 4194320 | tf_op jit(solution)/shard_map/all_gather | solution.py:161
  374.5 50.4 %all-gather.12.cloned.1.call-done = bf16[2048,1024]{1,0:T(8,128)(2,1)} async-done(((bf16[128,1024]{1,0:T(8,128)(2,1)}), bf16[2048,1024]{1,0:T(8,128)(2,1)}) %all-gather.12.cloned.1.call-update) | async-done | bytes 4194320 | tf_op jit(solution)/shard_map/all_gather | solution.py:162
  424.9 8.2 fusion.115
  433.2 52.4 %all-gather.14.cloned.1.call-done = bf16[1024,2048]{1,0:T(8,128)(2,1)} async-done(((bf16[1024,128]{1,0:T(8,128)(2,1)}), bf16[1024,2048]{1,0:T(8,128)(2,1)}) %all-gather.14.cloned.1.call-update) | async-done | bytes 4194320 | tf_op jit(solution)/shard_map/all_gather | solution.py:163
  485.5 8.9 multiply_convert_fusion.2
  503.4 143.9 %all-reduce.7.cloned.1.call-done = f32[768,2048]{1,0:T(8,128)} async-done(((f32[768,2048]{1,0:T(8,128)}), f32[768,2048]{1,0:T(8,128)}) %all-reduce.7.cloned.1.call-update) | async-done | bytes 6291472 | tf_op jit(solution)/shard_map/psum | solution.py:193
  662.1 126.4 %while.31 = (s32[]{:T(128)}, f32[4,768,64]{1,2,0:T(8,128)}, f32[4,3072,64]{1,2,0:T(8,128)}, f32[4,3072,64]{1,2,0:T(8,128)}, bf16[4,768,64]{2,1,0:T(8,128)(2,1)},...) while((s32[]{:T(128)}, f32[4,768,64]{1,2,0:T(8,128)}, ...), condition=%wide.region_17.18_spmd.clone.clone, body=%wide.region_15.17_spmd.clone.sunk.clone | while | flops 1538505984 | bytes 170169584 | solution.py:229
  665.5 7.4 multiply_reduce_fusion.6
  672.9 11.1 multiply_convert_fusion.7
  697.1 7.4 multiply_reduce_fusion.6
  704.5 11.1 multiply_convert_fusion.7
  728.7 7.4 multiply_reduce_fusion.6
  736.1 11.1 multiply_convert_fusion.7
  760.3 7.4 multiply_reduce_fusion.6
  767.7 11.1 multiply_convert_fusion.7
  806.0 23.6 %reduce-scatter.11.cloned.1.call-done = f32[768,1,128]{0,2,1:T(8,128)} async-done(((f32[3072,1,128]{0,2,1:T(8,128)}), f32[768,1,128]{0,2,1:T(8,128)}) %reduce-scatter.11.cloned.1.call-update) | async-done | bytes 393232 | tf_op jit(solution)/shard_map/reduce_scatter | solution.py:235
  834.1 9.1 fusion.120
  862.8 7.4 fusion.116
  875.4 29.5 %reduce-scatter.13.cloned.1.call-done = f32[128,256]{1,0:T(8,128)} async-done(((f32[2048,256]{1,0:T(8,128)}), f32[128,256]{1,0:T(8,128)}) %reduce-scatter.13.cloned.1.call-update) | async-done | bytes 131088 | tf_op jit(solution)/shard_map/reduce_scatter | solution.py:263
  906.6 73.1 %reduce-scatter.17.cloned.1.call-done = f32[256,128]{1,0:T(8,128)} async-done(((f32[256,2048]{1,0:T(8,128)}), f32[256,128]{1,0:T(8,128)}) %reduce-scatter.17.cloned.1.call-update) | async-done | bytes 131088 | tf_op jit(solution)/shard_map/reduce_scatter | solution.py:265
  981.4 68.5 %reduce-scatter.15.cloned.1.call-done = f32[128,1,128]{2,0,1:T(8,128)} async-done(((f32[2048,1,128]{2,0,1:T(8,128)}), f32[128,1,128]{2,0,1:T(8,128)}) %reduce-scatter.15.cloned.1.call-update) | async-done | bytes 65552 | tf_op jit(solution)/shard_map/reduce_scatter | solution.py:264
  1051.5 104.4 %reduce-scatter.21.cloned.1.call-done = f32[128,1024]{1,0:T(8,128)} async-done(((f32[2048,1024]{1,0:T(8,128)}), f32[128,1024]{1,0:T(8,128)}) %reduce-scatter.21.cloned.1.call-update) | async-done | bytes 524304 | tf_op jit(solution)/shard_map/reduce_scatter | solution.py:199
  1158.3 103.2 %reduce-scatter.19.cloned.1.call-done = f32[128,1024]{1,0:T(8,128)} async-done(((f32[2048,1024]{1,0:T(8,128)}), f32[128,1024]{1,0:T(8,128)}) %reduce-scatter.19.cloned.1.call-update) | async-done | bytes 524304 | tf_op jit(solution)/shard_map/reduce_scatter | solution.py:198
  1264.4 102.6 %reduce-scatter.23.cloned.1.call-done = f32[1024,128]{1,0:T(8,128)} async-done(((f32[1024,2048]{1,0:T(8,128)}), f32[1024,128]{1,0:T(8,128)}) %reduce-scatter.23.cloned.1.call-update) | async-done | bytes 524304 | tf_op jit(solution)/shard_map/reduce_scatter | solution.py:200
  1369.9 262.4 %all-reduce.9.cloned.1.call-done = (f32[768,2048]{1,0:T(8,128)}, f32[768,2048]{1,0:T(8,128)}) async-done(((f32[768,2048]{1,0:T(8,128)}, f32[768,2048]{1,0:T(8,128)}), (f32[768,2048]{1,0:T(8,128)}, f32[768,2048]{1,0:T(8,128)})) %all-reduce.9.cloned.1.call-update) | async-done | bytes 12582928 | tf_op jit(solution)/shard_map/psum | solution.py:171
  1637.6 13.2 fusion.57
  1650.8 52.5 %reduce-scatter.25.cloned.1.call-done = f32[128,2]{1,0:T(8,128)} async-done(((f32[2048,2]{1,0:T(8,128)}), f32[128,2]{1,0:T(8,128)}) %reduce-scatter.25.cloned.1.call-update) | async-done | bytes 1040
  (311 shorter events, 263.2 us)
Async XLA Ops:
  7.2 82.4 %all-gather.6.cloned.1.call-start = ((), (), s32[]{:S(2)}) async-start(), calls=%async_computation.8 | async-start | bytes 1114112 | tf_op jit(solution)/shard_map/all_gather | solution.py:111
  9.0 149.9 %all-gather.8.cloned.1.call-start = ((), (), s32[]{:S(2)}) async-start(), calls=%async_computation.9 | async-start | bytes 1114112 | tf_op jit(solution)/shard_map/all_gather | solution.py:113
  10.6 299.1 %all-reduce.5.cloned.1.call-start = ((), (), s32[]{:S(2)}) async-start(), calls=%async_computation.10 | async-start | bytes 12582912 | tf_op jit(solution)/shard_map/psum | solution.py:156
  164.0 203.3 %all-gather.10.cloned.1.call-start = ((), (), s32[]{:S(2)}) async-start(), calls=%async_computation.11 | async-start | bytes 4456448 | tf_op jit(solution)/shard_map/all_gather | solution.py:161
  165.9 259.1 %all-gather.12.cloned.1.call-start = ((), (), s32[]{:S(2)}) async-start(), calls=%async_computation.12 | async-start | bytes 4456448 | tf_op jit(solution)/shard_map/all_gather | solution.py:162
  167.7 317.8 %all-gather.14.cloned.1.call-start = ((), (), s32[]{:S(2)}) async-start(), calls=%async_computation.13 | async-start | bytes 4456448 | tf_op jit(solution)/shard_map/all_gather | solution.py:163
  169.6 146.5 %copy-start.40 = (f32[1,2048]{1,0:T(1,128)S(1)}, f32[1,2048]{1,0:T(1,128)}, u32[]{:S(2)}) copy-start(f32[1,2048]{1,0:T(1,128)} %get-tuple-element.412) | copy-start | bytes 24580
  169.6 477.6 %all-reduce.7.cloned.1.call-start = ((), (), s32[]{:S(2)}) async-start(), calls=%async_computation.14 | async-start | bytes 12582912 | tf_op jit(solution)/shard_map/psum | solution.py:193
  374.5 111.0 %copy-start.19 = (bf16[768,2048]{1,0:T(8,128)(2,1)S(1)}, bf16[768,2048]{1,0:T(8,128)(2,1)}, u32[]{:S(2)}) copy-start(bf16[768,2048]{1,0:T(8,128)(2,1)} %param.30) | copy-start | bytes 9437188
  503.3 326.4 %reduce-scatter.11.cloned.1.call-start = ((), (), s32[]{:S(2)}) async-start(), calls=%async_computation.15 | async-start | bytes 1966080 | tf_op jit(solution)/shard_map/reduce_scatter | solution.py:235
  795.6 109.2 %reduce-scatter.13.cloned.1.call-start = ((), (), s32[]{:S(2)}) async-start(), calls=%async_computation.16 | async-start | bytes 2228224 | tf_op jit(solution)/shard_map/reduce_scatter | solution.py:263
  800.5 179.2 %reduce-scatter.17.cloned.1.call-start = ((), (), s32[]{:S(2)}) async-start(), calls=%async_computation.18 | async-start | bytes 2228224 | tf_op jit(solution)/shard_map/reduce_scatter | solution.py:265
  806.0 244.0 %reduce-scatter.15.cloned.1.call-start = ((), (), s32[]{:S(2)}) async-start(), calls=%async_computation.17 | async-start | bytes 1114112 | tf_op jit(solution)/shard_map/reduce_scatter | solution.py:264
  834.0 321.8 %reduce-scatter.21.cloned.1.call-start = ((), (), s32[]{:S(2)}) async-start(), calls=%async_computation.20 | async-start | bytes 8912896 | tf_op jit(solution)/shard_map/reduce_scatter | solution.py:199
  843.3 418.2 %reduce-scatter.19.cloned.1.call-start = ((), (), s32[]{:S(2)}) async-start(), calls=%async_computation.19 | async-start | bytes 8912896 | tf_op jit(solution)/shard_map/reduce_scatter | solution.py:198
  852.3 514.7 %reduce-scatter.23.cloned.1.call-start = ((), (), s32[]{:S(2)}) async-start(), calls=%async_computation.21 | async-start | bytes 8912896 | tf_op jit(solution)/shard_map/reduce_scatter | solution.py:200
  861.4 770.9 %all-reduce.9.cloned.1.call-start = ((), (), s32[]{:S(2)}) async-start(), calls=%async_computation.23 | async-start | bytes 25165824 | tf_op jit(solution)/shard_map/psum | solution.py:171
  875.2 104.5 %copy-start.32 = (f32[256,128]{1,0:T(8,128)S(1)}, f32[256,128]{1,0:T(8,128)}, u32[]{:S(2)}) copy-start(f32[256,128]{1,0:T(8,128)} %param.39) | copy-start | bytes 393220
  875.2 104.5 %copy-start.38 = (f32[256,128]{1,0:T(8,128)S(1)}, f32[256,128]{1,0:T(8,128)}, u32[]{:S(2)}) copy-start(f32[256,128]{1,0:T(8,128)} %param.41) | copy-start | bytes 393220
  875.2 104.5 %copy-start.39 = (f32[256,128]{1,0:T(8,128)S(1)}, f32[256,128]{1,0:T(8,128)}, u32[]{:S(2)}) copy-start(f32[256,128]{1,0:T(8,128)} %param.40) | copy-start | bytes 393220
  875.2 174.7 %copy-start.35 = (f32[128,1,128]{2,1,0:T(1,128)S(1)}, f32[128,1,128]{2,1,0:T(1,128)}, u32[]{:S(2)}) copy-start(f32[128,1,128]{2,1,0:T(1,128)} %param.36) | copy-start | bytes 196612
  875.3 174.7 %copy-start.45 = (f32[128,1,128]{2,1,0:T(1,128)S(1)}, f32[128,1,128]{2,1,0:T(1,128)}, u32[]{:S(2)}) copy-start(f32[128,1,128]{2,1,0:T(1,128)} %param.38) | copy-start | bytes 196612
  875.3 174.7 %copy-start.46 = (f32[128,1,128]{2,1,0:T(1,128)S(1)}, f32[128,1,128]{2,1,0:T(1,128)}, u32[]{:S(2)}) copy-start(f32[128,1,128]{2,1,0:T(1,128)} %param.37) | copy-start | bytes 196612
  875.3 280.6 %copy-start.25 = (f32[128,1024]{1,0:T(8,128)S(1)}, f32[128,1024]{1,0:T(8,128)}, u32[]{:S(2)}) copy-start(f32[128,1024]{1,0:T(8,128)} %param.45) | copy-start | bytes 1572868
  875.3 280.5 %copy-start.29 = (f32[128,1024]{1,0:T(8,128)S(1)}, f32[128,1024]{1,0:T(8,128)}, u32[]{:S(2)}) copy-start(f32[128,1024]{1,0:T(8,128)} %param.47) | copy-start | bytes 1572868
  875.3 280.5 %copy-start.30 = (f32[128,1024]{1,0:T(8,128)S(1)}, f32[128,1024]{1,0:T(8,128)}, u32[]{:S(2)}) copy-start(f32[128,1024]{1,0:T(8,128)} %param.46) | copy-start | bytes 1572868
  875.3 828.0 %reduce-scatter.25.cloned.1.call-start = ((), (), s32[]{:S(2)}) async-start(), calls=%async_computation.22 | async-start | bytes 1114112
  1158.3 474.0 %copy-start.7 = (bf16[768,2048]{1,0:T(8,128)(2,1)S(1)}, bf16[768,2048]{1,0:T(8,128)(2,1)}, u32[]{:S(2)}) copy-start(bf16[768,2048]{1,0:T(8,128)(2,1)} %param.29) | copy-start | bytes 9437188
  1158.3 474.0 %copy-start.42 = (f32[1,2048]{1,0:T(1,128)S(1)}, f32[1,2048]{1,0:T(1,128)}, u32[]{:S(2)}) copy-start(f32[1,2048]{1,0:T(1,128)} %copy-done.41) | copy-start | bytes 24580
  1158.3 474.0 %copy-start.48 = (f32[768]{0:T(1024)S(1)}, f32[768]{0:T(1024)}, u32[]{:S(2)}) copy-start(f32[768]{0:T(1024)} %copy-done.47) | copy-start | bytes 9220
  1637.6 66.6 %copy-start.54 = (f32[2,128]{1,0:T(2,128)S(1)}, f32[2,128]{1,0:T(2,128)}, u32[]{:S(2)}) copy-start(f32[2,128]{1,0:T(2,128)} %param.51) | copy-start | bytes 3076
  1637.6 66.6 %copy-start.56 = (f32[2,128]{1,0:T(2,128)S(1)}, f32[2,128]{1,0:T(2,128)}, u32[]{:S(2)}) copy-start(f32[2,128]{1,0:T(2,128)} %param.52) | copy-start | bytes 3076
  (61 other events, 699.7 us)
Sparse Core Ops, SparseCore 0:
  11.0 48.7 all-gather.5
  62.6 44.4 all-gather.7
  164.1 145.5 all-reduce.4
  312.5 54.7 all-gather.9
  370.1 54.7 all-gather.11
  427.6 57.8 all-gather.13
  503.4 143.7 all-reduce.6
  795.8 33.8 reduce-scatter.10
  834.7 70.1 reduce-scatter.12
  909.8 69.9 reduce-scatter.16
  984.0 65.8 reduce-scatter.14
  1054.1 101.6 reduce-scatter.20
  1160.2 101.2 reduce-scatter.18
  1265.6 101.3 reduce-scatter.22
  1369.4 262.8 all-reduce.8
  1637.7 65.5 reduce-scatter.24
where the time goes:
time: 1720 us; the launch traced here: 1710 us
  waiting for transfers between devices  1260 us (73%)
  matrix products  204 us (12%)
  other arithmetic  128 us (7%)
  blocking collectives  55.8 us (3%)
  local copies, waits for them, and re-layouts  49.9 us (3%)
    psum x1, waiting for transfers between devices, per_device(): lax.psum(feedforward_term, 'tp')  262 us
    psum x1, waiting for transfers between devices, per_device(): d_normed_two = lax.psum(d_two_term, 'tp')  144 us
    psum x1, waiting for transfers between devices, per_device(): hidden_one = inputs + lax.psum(attention_term, 'tp')  140 us
    reduce_scatter x1, waiting for transfers between devices, per_device(): lax.psum_scatter(grad_up, ('shard', 'ctx'), scatter_dimension=0, tiled=True)  104 us
    reduce_scatter x1, waiting for transfers between devices, per_device(): lax.psum_scatter(grad_gate, ('shard', 'ctx'), scatter_dimension=0, tiled=...  103 us
    reduce_scatter x1, waiting for transfers between devices, per_device(): lax.psum_scatter(grad_down, ('shard', 'ctx'), scatter_dimension=1, tiled=...  103 us
    reduce_scatter x1, waiting for transfers between devices, per_device(): lax.psum_scatter(grad_out, ('shard', 'ctx'), scatter_dimension=1, tiled=T...  73.1 us
    reduce_scatter x1, waiting for transfers between devices, per_device(): lax.psum_scatter(grad_kv, ('shard', 'ctx'), scatter_dimension=0, tiled=True)  68.5 us
  transfers between devices with their start and end apart: 16, of which 14 were waited for; matrix products, arithmetic and copies ran while one was open for 11% of the time, Pallas kernels for 0%

commit v1 on v0

v1 whole, which is shorter than its diff:
```python
import functools

import jax
import jax.numpy as jnp
from jax import lax
from jax.experimental import pallas as pl
from jax.experimental.pallas import tpu as pltpu
from jax.sharding import Mesh
from jax.sharding import PartitionSpec as P

D = 2048
HD = 64
FF = 8192
STEP = 5


NORM_EPS = 1e-05
BETA_FIRST = 0.9
BETA_SECOND = 0.95
ADAM_EPS = 1e-08
DECAY_RATE = 0.1
ROPE_BASE = 500000.0
MASKED_SCORE = -1e30

F32 = jnp.float32
BF16 = jnp.bfloat16
SWAP = ((0, 1), (1, 0))


def ring(step):
    return tuple((i, (i + step) % 4) for i in range(4))


def layout_slots(lengths, groups, group_id, slot_ids):
    seq_count = lengths.shape[0]
    seq_order = jnp.arange(seq_count, dtype=jnp.int32)
    same_group = groups[None, :] == groups[:, None]
    before = seq_order[None, :] < seq_order[:, None]
    starts = jnp.sum(jnp.where(same_group & before, lengths[None, :], 0), axis=1)
    ends = starts + lengths
    inside = (
        (groups == group_id)[:, None]
        & (slot_ids[None, :] >= starts[:, None])
        & (slot_ids[None, :] < ends[:, None])
    )
    document = jnp.sum(jnp.where(inside, seq_order[:, None] + 1, 0), axis=0) - 1
    position = jnp.sum(jnp.where(inside, slot_ids[None, :] - starts[:, None], 0), axis=0)
    document = jnp.where(document < 0, seq_count + slot_ids, document)
    return (document, position)


def rotate(values, position, direction):
    half_dim = values.shape[-1] // 2
    frequency = ROPE_BASE ** (-2.0 * jnp.arange(half_dim, dtype=jnp.float32) / values.shape[-1])
    angles = position.astype(jnp.float32)[:, None] * frequency[None, :]
    cosine = jnp.cos(angles)[:, None, :]
    sine_part = direction * jnp.sin(angles)[:, None, :]
    first_half = values[..., :half_dim]
    second = values[..., half_dim:]
    return jnp.concatenate(
        [first_half * cosine - second * sine_part, second * cosine + first_half * sine_part],
        axis=-1,
    )


def adamw_step(weight, first, second, grad, rate, decay):
    first_new = BETA_FIRST * first + (1.0 - BETA_FIRST) * grad
    second_new = BETA_SECOND * second + (1.0 - BETA_SECOND) * grad * grad
    first_hat = first_new / (1.0 - BETA_FIRST**STEP)
    second_hat = second_new / (1.0 - BETA_SECOND**STEP)
    weight_new = weight - rate * (first_hat / (jnp.sqrt(second_hat) + ADAM_EPS) + decay * weight)
    return (first_new, second_new, weight_new)


def place(pieces, plan, table, out_shapes):
    moves = len(plan)
    size = sum(p.size * p.dtype.itemsize for p in pieces)

    def kernel(table_ref, *refs):
        sources, outs, sem = refs[: len(pieces)], refs[len(pieces) : -1], refs[-1]
        copies = []
        for n, (piece, source_index, out, entry) in enumerate(plan):
            source = sources[piece]
            if source_index is not None:
                source = source.at[source_index]
            copies.append(
                pltpu.make_async_copy(source, outs[out].at[table_ref[entry]], sem.at[n])
            )
        for copy in copies:
            copy.start()
        for copy in copies:
            copy.wait()

    return pl.pallas_call(
        kernel,
        out_shape=[jax.ShapeDtypeStruct(s, BF16) for s in out_shapes],
        in_specs=[pl.BlockSpec(memory_space=pltpu.SMEM)]
        + [pl.BlockSpec(memory_space=pl.ANY)] * len(pieces),
        out_specs=[pl.BlockSpec(memory_space=pl.ANY)] * len(out_shapes),
        scratch_shapes=[pltpu.SemaphoreType.DMA((moves,))],
        cost_estimate=pl.CostEstimate(flops=0, bytes_accessed=2 * size, transcendentals=0),
    )(table, *pieces)


def pick(blocks, axis, index):
    return lax.dynamic_index_in_dim(blocks, index, axis, keepdims=False)


class Here:
    def __init__(self):
        self.x, self.yh, self.c, self.yl, self.z = (
            lax.axis_index(a) for a in ("x", "yh", "c", "yl", "z")
        )

    def ztable(self):
        own = [self.yl * 4 + (self.z + k) % 4 for k in range(4)]
        other = [(1 - self.yl) * 4 + (self.z + k) % 4 for k in range(4)]
        return jnp.stack(own + other).astype(jnp.int32)

    def xtable(self):
        table = []
        for dc in range(2):
            core = self.c if dc == 0 else 1 - self.c
            for dy in range(2):
                yh = self.yh if dy == 0 else 1 - self.yh
                for k in range(4):
                    table.append(((self.x + k) % 4) * 4 + yh * 2 + core)
        return jnp.stack(table).astype(jnp.int32)

    def gather_tp(self, own, z_first, table):
        n, w = own.shape
        if not z_first:
            pair = jnp.stack([own, lax.ppermute(own, "yl", SWAP)])
            pieces = [pair] + [lax.ppermute(pair, "z", ring(-k)) for k in (1, 2, 3)]
            plan = [(k, d, 0, 4 * d + k) for k in range(4) for d in range(2)]
        else:
            mine = [own] + [lax.ppermute(own, "z", ring(-k)) for k in (1, 2, 3)]
            theirs = [lax.ppermute(p, "yl", SWAP) for p in mine]
            pieces = mine + theirs
            plan = [(i, None, 0, i) for i in range(8)]
        return place(pieces, plan, table, [(8, n, w)])[0].reshape(8 * n, w)

    def scatter_tp(self, terms, z_first):
        w = terms.shape[1]
        blocks = terms.reshape(2, 4, -1, w)
        if z_first:
            got = [
                lax.ppermute(pick(blocks, 1, (self.z + k) % 4), "z", ring(k)) for k in (1, 2, 3)
            ]
            keep = pick(pick(blocks, 1, self.z), 0, self.yl).astype(F32)
            give = pick(pick(blocks, 1, self.z), 0, 1 - self.yl).astype(F32)
            for g in got:
                keep = keep + pick(g, 0, self.yl).astype(F32)
                give = give + pick(g, 0, 1 - self.yl).astype(F32)
            return keep + lax.ppermute(give.astype(BF16), "yl", SWAP).astype(F32)
        got = lax.ppermute(pick(blocks, 0, 1 - self.yl), "yl", SWAP)
        both = pick(blocks, 0, self.yl).astype(F32) + got.astype(F32)
        low = both.astype(BF16)
        total = pick(both, 0, self.z)
        for k in (1, 2, 3):
            total = total + lax.ppermute(pick(low, 0, (self.z + k) % 4), "z", ring(k)).astype(F32)
        return total

    def gather_weights(self, shard):
        pair = jnp.stack([shard, lax.ppermute(shard, "yh", SWAP)])
        mine = [pair] + [lax.ppermute(pair, "x", ring(-k)) for k in (1, 2, 3)]
        return mine + [lax.ppermute(p, "c", SWAP) for p in mine]

    def scatter_weights(self, terms):
        w = terms.shape[1]
        blocks = terms.reshape(4, 2, 2, D // 16, w)
        got = lax.ppermute(pick(blocks, 2, 1 - self.c), "c", SWAP)
        both = pick(blocks, 2, self.c).astype(F32) + got.astype(F32)
        low = both.astype(BF16)
        total = pick(both, 0, self.x)
        for k in (1, 2, 3):
            total = total + lax.ppermute(pick(low, 0, (self.x + k) % 4), "x", ring(k)).astype(F32)
        give = pick(total, 0, 1 - self.yh).astype(BF16)
        return pick(total, 0, self.yh) + lax.ppermute(give, "yh", SWAP).astype(F32)

    def gather_ctx(self, own):
        over = lax.ppermute(own, "yh", SWAP)
        pieces = [own, over, lax.ppermute(own, "c", SWAP), lax.ppermute(over, "c", SWAP)]
        table = jnp.stack(
            [
                self.yh * 2 + self.c,
                (1 - self.yh) * 2 + self.c,
                self.yh * 2 + 1 - self.c,
                (1 - self.yh) * 2 + 1 - self.c,
            ]
        ).astype(jnp.int32)
        n, w = own.shape
        plan = [(i, None, 0, i) for i in range(4)]
        return place(pieces, plan, table, [(4, n, w)])[0].reshape(4 * n, w)

    def scatter_ctx(self, terms):
        w = terms.shape[1]
        blocks = terms.reshape(2, 2, -1, w)
        got = lax.ppermute(pick(blocks, 1, 1 - self.c).astype(BF16), "c", SWAP)
        both = pick(blocks, 1, self.c) + got.astype(F32)
        give = pick(both, 0, 1 - self.yh).astype(BF16)
        return pick(both, 0, self.yh) + lax.ppermute(give, "yh", SWAP).astype(F32)

    def sum_tp(self, value):
        value = value + lax.ppermute(value, "yl", SWAP)
        got = [lax.ppermute(value, "z", ring(k)) for k in (1, 2, 3)]
        parts = jnp.stack([value] + got)
        order = jnp.stack([(self.z - j) % 4 for j in range(4)])
        return jnp.sum(jnp.take(parts, order, axis=0), axis=0)


def per_device(
    tokens,
    cotangent,
    lengths,
    groups,
    query_weight,
    query_m,
    query_v,
    kv_weight,
    kv_m,
    kv_v,
    out_weight,
    out_m,
    out_v,
    gate_weight,
    gate_m,
    gate_v,
    up_weight,
    up_m,
    up_v,
    down_weight,
    down_m,
    down_v,
    norm_gains,
    gains_m,
    gains_v,
):
    here = Here()
    row_count = tokens.shape[0]
    group_rows = row_count * 4
    group_id = here.x
    ctx_id = here.yh * 2 + here.c
    tp_id = here.yl * 4 + here.z
    half = row_count // 2
    part = half // 8
    scale = HD ** (-0.5)
    ztable = here.ztable()
    xtable = here.xtable()

    kv_flat = kv_weight.reshape(D // 16, 2 * HD)
    attn_shard = jnp.concatenate([query_weight, kv_flat, out_weight.T], axis=1).astype(BF16)
    q_cols, kv_cols, o_cols = query_weight.shape[1], 2 * HD, out_weight.shape[0]
    cols = q_cols + kv_cols + o_cols
    gains_low = norm_gains.astype(BF16)
    gain_rows = jnp.zeros((16, cols), BF16).at[:2, : D // 16].set(gains_low)
    attn_pieces = here.gather_weights(jnp.concatenate([attn_shard, gain_rows], axis=0))
    plan = []
    for i in range(8):
        for d in range(2):
            entry = (i // 4) * 8 + d * 4 + i % 4
            rows = pl.ds(0, D // 16)
            plan.append((i, (d, rows, pl.ds(0, q_cols)), 0, entry))
            plan.append((i, (d, rows, pl.ds(q_cols, kv_cols)), 1, entry))
            plan.append((i, (d, rows, pl.ds(q_cols + kv_cols, o_cols)), 2, entry))
            plan.append((i, (d, pl.ds(D // 16, 16), pl.ds(0, D // 16)), 3, entry))
    w_query, w_kv, w_out, gain_blocks = place(
        attn_pieces,
        plan,
        xtable,
        [(16, D // 16, q_cols), (16, D // 16, kv_cols), (16, D // 16, o_cols), (16, 16, D // 16)],
    )
    w_query = w_query.reshape(D, q_cols)
    w_kv = w_kv.reshape(D, kv_cols)
    w_out = w_out.reshape(D, o_cols)
    gain_values = gain_blocks[:, :2].transpose(1, 0, 2).reshape(2, D).astype(F32)

    units = gate_weight.shape[1]
    ff_shard = jnp.stack([gate_weight, up_weight, down_weight.T]).astype(BF16)
    ff_shard, _ = lax.optimization_barrier((ff_shard, attn_pieces[1]))
    ff_pieces = here.gather_weights(ff_shard)
    plan = []
    for i in range(8):
        for d in range(2):
            for o in range(3):
                plan.append((i, (d, o), o, (i // 4) * 8 + d * 4 + i % 4))
    w_gate, w_up, w_down = (
        w.reshape(D, units) for w in place(ff_pieces, plan, xtable, [(16, D // 16, units)] * 3)
    )

    key_doc, key_pos = layout_slots(
        lengths, groups, group_id, jnp.arange(group_rows, dtype=jnp.int32)
    )
    own_doc, own_pos = layout_slots(
        lengths, groups, group_id, ctx_id * row_count + jnp.arange(row_count, dtype=jnp.int32)
    )
    visible = (own_doc[:, None] == key_doc[None, :]) & (key_pos[None, :] <= own_pos[:, None])

    inputs = tokens.astype(F32)
    inv_one = lax.rsqrt(jnp.mean(inputs * inputs, axis=-1, keepdims=True) + NORM_EPS)
    normed_one = (inputs * inv_one * gain_values[0]).astype(BF16)
    head_count = q_cols // HD
    kv_raw = jnp.dot(normed_one, w_kv, preferred_element_type=F32).reshape(row_count, 1, 2 * HD)
    kv_local = jnp.concatenate(
        [rotate(kv_raw[..., :HD], own_pos, 1.0), kv_raw[..., HD:]], axis=-1
    ).astype(BF16)
    kv_whole = here.gather_ctx(kv_local.reshape(row_count, 2 * HD))
    key_head, value_head = kv_whole[:, :HD], kv_whole[:, HD:]
    query_raw = jnp.dot(normed_one, w_query, preferred_element_type=F32).reshape(
        row_count, head_count, HD
    )
    queries = rotate(query_raw, own_pos, 1.0).astype(BF16).transpose(1, 0, 2)

    def forward_head(query_head):
        scores = (
            jnp.einsum("rd,kd->rk", query_head, key_head, preferred_element_type=F32) * scale
        )
        scores = jnp.where(visible, scores, MASKED_SCORE)
        row_peak = jnp.max(scores, axis=-1, keepdims=True)
        powers = jnp.exp(scores - row_peak)
        summed = jnp.sum(powers, axis=-1, keepdims=True)
        chances = (powers / summed).astype(BF16)
        mixed_head = jnp.dot(chances, value_head, preferred_element_type=F32)
        return (mixed_head, (row_peak + jnp.log(summed))[:, 0])

    mixed_heads, log_totals = lax.map(forward_head, queries)
    mixed = mixed_heads.transpose(1, 0, 2).reshape(row_count, head_count * HD).astype(BF16)

    halves = (0, 1)
    z_first = (False, True)
    mixed_half = [mixed[:half], mixed[half:]]
    cotangent_half = [cotangent[:half], cotangent[half:]]
    own_start = [h * half + tp_id * part for h in halves]
    own_inputs = [
        lax.dynamic_slice_in_dim(tokens, s, part, axis=0).astype(F32) for s in own_start
    ]
    own_upstream = [
        lax.dynamic_slice_in_dim(cotangent, s, part, axis=0).astype(F32) for s in own_start
    ]

    hidden_one, inv_two, pre_two, normed_two = [], [], [], []
    for h in halves:
        term = jnp.einsum("ra,da->rd", mixed_half[h], w_out, preferred_element_type=F32)
        total = here.scatter_tp(term.astype(BF16), z_first[h])
        hidden_one.append(own_inputs[h] + total)
        inv_two.append(
            lax.rsqrt(jnp.mean(hidden_one[h] * hidden_one[h], axis=-1, keepdims=True) + NORM_EPS)
        )
        pre_two.append(hidden_one[h] * inv_two[h])
        own_normed = (pre_two[h] * gain_values[1]).astype(BF16)
        normed_two.append(here.gather_tp(own_normed, z_first[h], ztable))

    hidden, d_gate, d_up, d_hidden_one, d_branch = [], [], [], [], []
    for h in halves:
        gate_value = jnp.dot(normed_two[h], w_gate, preferred_element_type=F32)
        up_value = jnp.dot(normed_two[h], w_up, preferred_element_type=F32)
        d_hidden = jnp.dot(cotangent_half[h], w_down, preferred_element_type=F32)
        sigmoid_gate = jax.nn.sigmoid(gate_value)
        activated = gate_value * sigmoid_gate
        hidden.append((activated * up_value).astype(BF16))
        d_gate.append(
            (
                d_hidden * up_value * sigmoid_gate * (1.0 + gate_value * (1.0 - sigmoid_gate))
            ).astype(BF16)
        )
        d_up.append((d_hidden * activated).astype(BF16))
        d_two_term = jnp.einsum(
            "rf,df->rd", d_gate[h], w_gate, preferred_element_type=F32
        ) + jnp.einsum("rf,df->rd", d_up[h], w_up, preferred_element_type=F32)
        d_normed_two = here.scatter_tp(d_two_term.astype(BF16), z_first[h])
        scaled = d_normed_two * gain_values[1]
        d_through = inv_two[h] * (
            scaled - pre_two[h] * jnp.mean(scaled * pre_two[h], axis=-1, keepdims=True)
        )
        d_hidden_one.append(own_upstream[h] + d_through)
        d_branch.append(
            here.gather_tp(d_hidden_one[h].astype(BF16), z_first[h], ztable)
        )

    d_mixed = jnp.concatenate(
        [jnp.dot(d_branch[h], w_out, preferred_element_type=F32).astype(BF16) for h in halves]
    )

    outputs = []
    for h in halves:
        term = jnp.einsum("rf,df->rd", hidden[h], w_down, preferred_element_type=F32)
        total = here.scatter_tp(term.astype(BF16), z_first[h])
        own_out = (hidden_one[h] + total).astype(BF16)
        outputs.append(here.gather_tp(own_out, z_first[h], ztable))
    output = jnp.concatenate(outputs)

    both = lambda pair: jnp.concatenate(pair, axis=0)
    normed_two_all = both(normed_two)
    outer = lambda a, b: jnp.einsum("rd,rf->df", a, b, preferred_element_type=F32).astype(BF16)
    grad_gate = here.scatter_weights(outer(normed_two_all, both(d_gate)))
    grad_up = here.scatter_weights(outer(normed_two_all, both(d_up)))
    grad_down = here.scatter_weights(outer(cotangent, both(hidden))).T

    d_mixed = d_mixed.reshape(row_count, head_count, HD).transpose(1, 0, 2)

    def backward_head(operands):
        query_head, d_head, log_total = operands
        scores = (
            jnp.einsum("rd,kd->rk", query_head, key_head, preferred_element_type=F32) * scale
        )
        scores = jnp.where(visible, scores, MASKED_SCORE)
        chances = jnp.exp(scores - log_total[:, None])
        d_value = jnp.einsum("rk,rd->kd", chances.astype(BF16), d_head, preferred_element_type=F32)
        d_chances = jnp.einsum("rd,kd->rk", d_head, value_head, preferred_element_type=F32)
        centre = jnp.sum(chances * d_chances, axis=-1, keepdims=True)
        d_scores = (chances * (d_chances - centre)).astype(BF16)
        d_query = jnp.dot(d_scores, key_head, preferred_element_type=F32) * scale
        d_key = jnp.einsum("rk,rd->kd", d_scores, query_head, preferred_element_type=F32) * scale
        return (d_query, d_key, d_value)

    d_queries, d_keys, d_values = lax.map(backward_head, (queries, d_mixed, log_totals))
    d_kv = jnp.concatenate([d_keys.sum(axis=0), d_values.sum(axis=0)], axis=-1)
    d_kv_own = here.scatter_ctx(d_kv)[:, None]
    d_kv_low = (
        jnp.concatenate([rotate(d_kv_own[..., :HD], own_pos, -1.0), d_kv_own[..., HD:]], axis=-1)
        .astype(BF16)
        .reshape(row_count, 2 * HD)
    )
    d_query_low = (
        rotate(d_queries.transpose(1, 0, 2), own_pos, -1.0)
        .astype(BF16)
        .reshape(row_count, head_count * HD)
    )

    tokens_grads = []
    for h in halves:
        rows = slice(h * half, (h + 1) * half)
        d_one_term = jnp.einsum(
            "ra,da->rd", d_query_low[rows], w_query, preferred_element_type=F32
        ) + jnp.einsum("rc,dc->rd", d_kv_low[rows], w_kv, preferred_element_type=F32)
        d_normed_one = here.scatter_tp(d_one_term.astype(BF16), z_first[h])
        own_inv = lax.rsqrt(
            jnp.mean(own_inputs[h] * own_inputs[h], axis=-1, keepdims=True) + NORM_EPS
        )
        pre_one = own_inputs[h] * own_inv
        scaled = d_normed_one * gain_values[0]
        d_through = own_inv * (
            scaled - pre_one * jnp.mean(scaled * pre_one, axis=-1, keepdims=True)
        )
        own_grad = (d_hidden_one[h] + d_through).astype(BF16)
        tokens_grads.append(here.gather_tp(own_grad, z_first[h], ztable))
    tokens_grad = jnp.concatenate(tokens_grads)

    grad_attn = here.scatter_weights(
        jnp.concatenate(
            [
                outer(normed_one, d_query_low),
                outer(normed_one, d_kv_low),
                outer(both(d_branch), mixed),
            ],
            axis=1,
        )
    )
    grad_query = grad_attn[:, :q_cols]
    grad_kv_flat = grad_attn[:, q_cols : q_cols + kv_cols]
    grad_out = grad_attn[:, q_cols + kv_cols :].T

    low = lambda w: w.astype(BF16).astype(F32)
    gain_one = jnp.sum(low(query_weight) * grad_query, axis=1) + jnp.sum(
        low(kv_flat) * grad_kv_flat, axis=1
    )
    gain_two = jnp.sum(low(gate_weight) * grad_gate + low(up_weight) * grad_up, axis=1)
    grad_gains = here.sum_tp(jnp.stack([gain_one, gain_two])) / gains_low.astype(F32)
    grad_kv = grad_kv_flat.reshape(kv_weight.shape)

    out_fan = max(1, 4 * D // group_rows)
    query_new = adamw_step(query_weight, query_m, query_v, grad_query, D ** (-0.5), DECAY_RATE)
    kv_new = adamw_step(kv_weight, kv_m, kv_v, grad_kv, D ** (-0.5), DECAY_RATE)
    out_new = adamw_step(out_weight, out_m, out_v, grad_out, out_fan ** (-0.5), DECAY_RATE)
    gate_new = adamw_step(gate_weight, gate_m, gate_v, grad_gate, D ** (-0.5), DECAY_RATE)
    up_new = adamw_step(up_weight, up_m, up_v, grad_up, D ** (-0.5), DECAY_RATE)
    down_new = adamw_step(down_weight, down_m, down_v, grad_down, FF ** (-0.5), DECAY_RATE)
    gains_new = adamw_step(norm_gains, gains_m, gains_v, grad_gains, 0.5, 0.0)
    return (
        output,
        tokens_grad,
        *query_new,
        *kv_new,
        *out_new,
        *gate_new,
        *up_new,
        *down_new,
        *gains_new,
    )


def solution(mesh):
    fine = Mesh(mesh.devices.reshape(4, 2, 2, 2, 4), ("x", "yh", "c", "yl", "z"))
    rows = ("x", "yh", "c")
    tp = ("yl", "z")
    by_row, by_col, by_unit = P(rows, None), P(rows, tp), P(tp, rows)
    by_kv, by_gain = P(rows, tp, None), P(None, rows)
    in_specs = (
        (by_row,) * 2
        + (P(),) * 2
        + (by_col,) * 3
        + (by_kv,) * 3
        + (by_unit,) * 3
        + (by_col,) * 6
        + (by_unit,) * 3
        + (by_gain,) * 3
    )
    out_specs = (
        (by_row,) * 2
        + (by_col,) * 3
        + (by_kv,) * 3
        + (by_unit,) * 3
        + (by_col,) * 6
        + (by_unit,) * 3
        + (by_gain,) * 3
    )
    return jax.shard_map(
        per_device, mesh=fine, in_specs=in_specs, out_specs=out_specs, check_vma=False
    )
```

time: 1720 us -> 1700 us (0.988)
  waiting for transfers between devices: 1260 us -> 189 us
  Pallas kernels: 0 us -> 889 us
  starting transfers between devices: 1.41 us -> 175 us
  local copies, waits for them, and re-layouts: 49.9 us -> 132 us
  blocking collectives: 55.8 us -> 0 us
  matrix products: 204 us -> 161 us
    pallas_call x0 -> x11, Pallas kernels: none -> 889 us  [place(): pl.pallas_call(kernel, out_shape=[jax.ShapeDtypeStruct(s, BF16) for s in...]
    psum x3 -> x0, waiting for transfers between devices: 546 us -> none  [the longest x1 262 us: per_device(): lax.psum(feedforward_term, 'tp')]
    reduce_scatter x7 -> x0, waiting for transfers between devices: 505 us -> none  [the longest x1 104 us: per_device(): lax.psum_scatter(grad_up, ('shard', 'ctx'), scatter_dimension=0, tiled=True)]
    ppermute x0 -> x121, waiting for transfers between devices: none -> 189 us  [the longest x6 54.8 us: gather_weights(): mine = [pair] + [lax.ppermute(pair, 'x', ring(-k)) for k in (1, 2, 3)]]
    ppermute x0 -> x121, starting transfers between devices: none -> 175 us  [the longest x12 26.2 us: gather_tp(): pieces = [pair] + [lax.ppermute(pair, 'z', ring(-k)) for k in (1, 2, 3)]]
    all_gather x5 -> x0, waiting for transfers between devices: 153 us -> none  [the longest x1 52.4 us: per_device(): lax.all_gather(down_weight.astype(jnp.bfloat16), ('shard', 'ctx'), axis=1...]
    all_gather x3 -> x0, blocking collectives: 55.8 us -> none  [the longest x1 24.3 us: per_device(): lax.all_gather(norm_gains.astype(jnp.bfloat16), ('shard', 'ctx'), axis=1,...]
    unnamed x17 -> x0, waiting for transfers between devices: 52.7 us -> none
  transfers between devices with their start and end apart: 16 -> 121, of which waited for: 14 -> 40; matrix products, arithmetic and copies ran while one was open for 11% -> 19% of each run, Pallas kernels for 0% -> 23%
where the time goes in v1:
time: 1700 us; the launch traced here: 1690 us
  Pallas kernels  889 us (52%)
  waiting for transfers between devices  189 us (11%)
  starting transfers between devices  175 us (10%)
  matrix products  161 us (9%)
  other arithmetic  139 us (8%)
  local copies, waits for them, and re-layouts  132 us (8%)
    pallas_call x11, Pallas kernels, place(): pl.pallas_call(kernel, out_shape=[jax.ShapeDtypeStruct(s, BF16) for s in...  889 us
    ppermute x6, waiting for transfers between devices, gather_weights(): mine = [pair] + [lax.ppermute(pair, 'x', ring(-k)) for k in (1, 2, 3)]  54.8 us
    unnamed x350, local copies, waits for them, and re-layouts  50.4 us
    convert_element_type x4, other arithmetic, backward_head(): d_scores = (chances * (d_chances - centre)).astype(BF16)  44.5 us
  transfers between devices with their start and end apart: 121, of which 40 were waited for; matrix products, arithmetic and copies ran while one was open for 19% of the time, Pallas kernels for 23%

profile of v1, /device:TPU:0, one launch (start us, length us, event | category | flops | bytes accessed | tf_op | source)
XLA Modules:
  0.0 1689.2 jit_solution(5769469174460576305)
XLA Ops:
  18.7 11.4 collective-permute-done.1.refs_1_
  36.3 83.8 %shard_map.416 = (bf16[16,128,256]{2,1,0:T(8,128)(2,1)}, bf16[16,128,128]{2,1,0:T(8,128)(2,1)}, bf16[16,128,256]{2,1,0:T(8,128)(2,1)}, bf16[16,16,128]{2,1,0:T(8,128)(2,1)}) custom-call(s32[16]{0:T(128)} %stack.235.table_ref, bf16[2,144,640]{2,1,0:T(8,128)(2,1)} %copy-done.57, bf16[2,144,640]{2,1,0:T(8,128)(2,1)} %copy-done.96, ...), custom_call_target="tpu_custom_call" | custom-call | bytes 5898240 | tf_op jit(solution)/shard_map/pallas_call | solution.py:94
  137.9 25.6 %shard_map.417 = bf16[4,768,128]{2,1,0:T(8,128)(2,1)} custom-call(s32[4]{0:T(128)} %pad_add_fusion.table_ref, bf16[768,128]{1,0:T(8,128)(2,1)} %copy-done.73, bf16[768,128]{1,0:T(8,128)(2,1)} %collective-permute-done.8.refs_1_, bf16[768,128]{1,0:T(8,128)(2,1)} %collective-permute-done.9.refs_2_, bf16[768,128]{1,0:T(8,128)(2,1)} %copy-done.103), custom_call_target="tpu_custom_call" | custom-call | bytes 1572864 | tf_op jit(solution)/shard_map/pallas_call | solution.py:94
  165.3 54.8 %while.31 = (s32[]{:T(128)}, bf16[4,768,64]{1,2,0:T(8,128)(2,1)}, f32[4,768]{1,0:T(4,128)}, bf16[4,768,64]{2,1,0:T(8,128)(2,1)S(1)}, bf16[3072,64]{1,0:T(8,128)(...) while((s32[]{:T(128)}, bf16[4,768,64]{1,2,0:T(8,128)(2,1)}, ...), condition=%wide.region_9.10_spmd.clone.clone, body=%wide.region_6.9_spmd.clone.sunk.clone | while | flops 629931264 | bytes 67703432 | solution.py:326
  238.0 9.6 collective-permute-done.36
  305.0 31.0 %collective-permute-done.22.refs_3_ = bf16[2,3,128,1024]{3,2,1,0:T(8,128)(2,1)} collective-permute-done((bf16[2,3,128,1024]{3,2,1,0:T(8,128)(2,1)S(1)}, bf16[2,3,128,1024]{3,2,1,0:T(8,128)(2,1)}, u32[]{:S(2)}, u32[]{:S(2)}) %collective-permute-start.22) | collective-permute-done | bytes 1572896 | tf_op jit(solution)/shard_map/ppermute | solution.py:166
  347.3 8.5 collective-permute-done.16.refs_1_
  372.2 49.5 %shard_map.421 = bf16[8,48,2048]{2,1,0:T(8,128)(2,1)} custom-call(s32[8]{0:T(128)} %stack.218.table_ref, bf16[48,2048]{1,0:T(8,128)(2,1)} %copy-done.76, bf16[48,2048]{1,0:T(8,128)(2,1)} %copy-done.104, bf16[48,2048]{1,0:T(8,128)(2,1)} %copy-done.105, bf16[48,2048]{1,0:T(8,128)(2,1)} %copy-done.106, bf16[48,2048]{1,0:T(8,128)(2,1)} %copy-done.107, ...), custom_call_target="tpu_custom_call" | custom-call | bytes 3145728 | tf_op jit(solution)/shard_map/pallas_call | solution.py:94
  421.7 49.5 %shard_map.418 = bf16[8,48,2048]{2,1,0:T(8,128)(2,1)} custom-call(s32[8]{0:T(128)} %stack.218.table_ref, bf16[2,48,2048]{2,1,0:T(8,128)(2,1)} %pad_maximum_fusion.9.refs_0_, bf16[2,48,2048]{2,1,0:T(8,128)(2,1)} %collective-permute-done.16.refs_1_, bf16[2,48,2048]{2,1,0:T(8,128)(2,1)} %collective-permute-done.17.refs_2_, ...), custom_call_target="tpu_custom_call" | custom-call | bytes 3145728 | tf_op jit(solution)/shard_map/pallas_call | solution.py:94
  471.2 383.5 %shard_map.419 = (bf16[16,128,1024]{2,1,0:T(8,128)(2,1)}, bf16[16,128,1024]{2,1,0:T(8,128)(2,1)}, bf16[16,128,1024]{2,1,0:T(8,128)(2,1)}) custom-call(s32[16]{0:T(128)} %stack.235.table_ref, bf16[2,3,128,1024]{3,2,1,0:T(8,128)(2,1)} %copy-done.9, bf16[2,3,128,1024]{3,2,1,0:T(8,128)(2,1)} %collective-permute-done.20.refs_1_, ...), custom_call_target="tpu_custom_call" | custom-call | bytes 25165824 | tf_op jit(solution)/shard_map/pallas_call | solution.py:94
  901.6 7.7 reshape.850
  909.3 11.5 constant_dynamic-slice_fusion.1
  929.1 10.8 collective-permute-done.46
  982.9 10.6 copy.228
  993.4 10.6 copy.227
  1033.8 49.6 %shard_map.424 = bf16[8,48,2048]{2,1,0:T(8,128)(2,1)} custom-call(s32[8]{0:T(128)} %stack.218.table_ref, bf16[48,2048]{1,0:T(8,128)(2,1)} %copy-done.79, bf16[48,2048]{1,0:T(8,128)(2,1)} %copy-done.111, bf16[48,2048]{1,0:T(8,128)(2,1)} %copy-done.113, bf16[48,2048]{1,0:T(8,128)(2,1)} %copy-done.115, bf16[48,2048]{1,0:T(8,128)(2,1)} %copy-done.119, ...), custom_call_target="tpu_custom_call" | custom-call | bytes 3145728 | tf_op jit(solution)/shard_map/pallas_call | solution.py:94
  1084.0 49.5 %shard_map.422 = bf16[8,48,2048]{2,1,0:T(8,128)(2,1)} custom-call(s32[8]{0:T(128)} %stack.218.table_ref, bf16[48,2048]{1,0:T(8,128)(2,1)} %copy-done.78, bf16[48,2048]{1,0:T(8,128)(2,1)} %collective-permute-done.50.refs_1_, bf16[48,2048]{1,0:T(8,128)(2,1)} %copy-done.117, bf16[48,2048]{1,0:T(8,128)(2,1)} %copy-done.118, bf16[48,2048]{1,0:T(8,128)(2,1)} %copy-done.123, ...), custom_call_target="tpu_custom_call" | custom-call | bytes 3145728 | tf_op jit(solution)/shard_map/pallas_call | solution.py:94
  1140.4 49.5 %shard_map.423 = bf16[8,48,2048]{2,1,0:T(8,128)(2,1)} custom-call(s32[8]{0:T(128)} %stack.218.table_ref, bf16[2,48,2048]{2,1,0:T(8,128)(2,1)} %copy-done.54, bf16[2,48,2048]{2,1,0:T(8,128)(2,1)} %copy-done.94, bf16[2,48,2048]{2,1,0:T(8,128)(2,1)} %collective-permute-done.63.refs_2_, bf16[2,48,2048]{2,1,0:T(8,128)(2,1)} %collective-permute-done.64.refs_3_), custom_call_target="tpu_custom_call" | custom-call | bytes 3145728 | tf_op jit(solution)/shard_map/pallas_call | solution.py:94
  1192.3 115.1 %while.32 = (s32[]{:T(128)}, f32[4,768,64]{1,2,0:T(8,128)}, f32[4,3072,64]{1,2,0:T(8,128)}, f32[4,3072,64]{1,2,0:T(8,128)}, bf16[4,768,64]{2,1,0:T(8,128)(2,1)S(...) while((s32[]{:T(128)}, f32[4,768,64]{1,2,0:T(8,128)}, ...), condition=%wide.region_17.18_spmd.clone.clone, body=%wide.region_15.17_spmd.clone.sunk.clone | while | flops 1538505984 | bytes 169528016 | solution.py:416
  1201.3 11.1 multiply_convert_fusion.7
  1230.1 11.1 multiply_convert_fusion.7
  1258.9 11.1 multiply_convert_fusion.7
  1287.7 11.1 multiply_convert_fusion.7
  1316.8 49.5 %shard_map.420 = bf16[8,48,2048]{2,1,0:T(8,128)(2,1)} custom-call(s32[8]{0:T(128)} %stack.218.table_ref, bf16[2,48,2048]{2,1,0:T(8,128)(2,1)} %pad_maximum_fusion.10.refs_0_, bf16[2,48,2048]{2,1,0:T(8,128)(2,1)} %collective-permute-done.32.refs_1_, bf16[2,48,2048]{2,1,0:T(8,128)(2,1)} %collective-permute-done.33.refs_2_, ...), custom_call_target="tpu_custom_call" | custom-call | bytes 3145728 | tf_op jit(solution)/shard_map/pallas_call | solution.py:94
  1413.8 7.7 constant_dynamic-slice_fusion.3
  1425.6 7.3 collective-permute-done.87
  1462.2 10.9 collective-permute-done.115
  1483.1 9.1 collective-permute-done.110
  1496.1 11.3 collective-permute-done.116
  1552.4 9.7 collective-permute-start.100
  1568.2 49.5 %shard_map.426 = bf16[8,48,2048]{2,1,0:T(8,128)(2,1)} custom-call(s32[8]{0:T(128)} %stack.218.table_ref, bf16[48,2048]{1,0:T(8,128)(2,1)} %copy-done.77, bf16[48,2048]{1,0:T(8,128)(2,1)} %copy-done.120, bf16[48,2048]{1,0:T(8,128)(2,1)} %copy-done.121, bf16[48,2048]{1,0:T(8,128)(2,1)} %copy-done.122, bf16[48,2048]{1,0:T(8,128)(2,1)} %copy-done.124, ...), custom_call_target="tpu_custom_call" | custom-call | bytes 3145728 | tf_op jit(solution)/shard_map/pallas_call | solution.py:94
  1617.8 49.6 %shard_map.425 = bf16[8,48,2048]{2,1,0:T(8,128)(2,1)} custom-call(s32[8]{0:T(128)} %stack.218.table_ref, bf16[2,48,2048]{2,1,0:T(8,128)(2,1)} %copy-done.53, bf16[2,48,2048]{2,1,0:T(8,128)(2,1)} %copy-done.93, bf16[2,48,2048]{2,1,0:T(8,128)(2,1)} %collective-permute-done.84.refs_2_, bf16[2,48,2048]{2,1,0:T(8,128)(2,1)} %collective-permute-done.85.refs_3_), custom_call_target="tpu_custom_call" | custom-call | bytes 3145728 | tf_op jit(solution)/shard_map/pallas_call | solution.py:94
  (829 shorter events, 584.4 us)
Async XLA Ops:
  265.9 39.1 %collective-permute-start.21 = (bf16[2,3,128,1024]{3,2,1,0:T(8,128)(2,1)S(1)}, bf16[2,3,128,1024]{3,2,1,0:T(8,128)(2,1)}, u32[]{:S(2)}, u32[]{:S(2)}) collective-permute-start(bf16[2,3,128,1024]{3,2,1,0:T(8,128)(2,1)S(1)} %pad_maximum_fusion.6.refs_0_), channel_id=1, source_target_pairs={{0,64},{32,96},{64,0},{96,32},{1,65},{33,97},{65,1},{97,33},{2,66}... | collective-permute-start | bytes 4718600 | tf_op jit(solution)/shard_map/ppermute | solution.py:166
  266.8 69.1 %collective-permute-start.22 = (bf16[2,3,128,1024]{3,2,1,0:T(8,128)(2,1)S(1)}, bf16[2,3,128,1024]{3,2,1,0:T(8,128)(2,1)}, u32[]{:S(2)}, u32[]{:S(2)}) collective-permute-start(bf16[2,3,128,1024]{3,2,1,0:T(8,128)(2,1)S(1)} %pad_maximum_fusion.6.refs_0_), channel_id=1, source_target_pairs={{0,32},{32,64},{64,96},{96,0},{1,33},{33,65},{65,97},{97,1},{2,34}... | collective-permute-start | bytes 4718600 | tf_op jit(solution)/shard_map/ppermute | solution.py:166
  293.2 42.8 %collective-permute-start.44 = (bf16[48,2048]{1,0:T(8,128)(2,1)S(1)}, bf16[48,2048]{1,0:T(8,128)(2,1)S(1)}, u32[]{:S(2)}, u32[]{:S(2)}) collective-permute-start(bf16[48,2048]{1,0:T(8,128)(2,1)S(1)} %collective-permute-done.40.refs_2_), channel_id=1, source_target_pairs={{0,4},{4,0},{1,5},{5,1},{2,6},{6,2},{3,7},{7,3},{8,12},{12,8},{9,1... | collective-permute-start | bytes 589832 | tf_op jit(solution)/shard_map/ppermute | solution.py:138
  295.7 175.5 %collective-permute-start.23 = (bf16[2,3,128,1024]{3,2,1,0:T(8,128)(2,1)S(1)}, bf16[2,3,128,1024]{3,2,1,0:T(8,128)(2,1)}, u32[]{:S(2)}, u32[]{:S(2)}) collective-permute-start(bf16[2,3,128,1024]{3,2,1,0:T(8,128)(2,1)S(1)} %pad_maximum_fusion.6.refs_0_), channel_id=1, source_target_pairs={{0,8},{8,0},{1,9},{9,1},{2,10},{10,2},{3,11},{11,3},{4,12},{12,4},... | collective-permute-start | bytes 4718600 | tf_op jit(solution)/shard_map/ppermute | solution.py:167
  302.7 168.5 %collective-permute-start.24 = (bf16[2,3,128,1024]{3,2,1,0:T(8,128)(2,1)}, bf16[2,3,128,1024]{3,2,1,0:T(8,128)(2,1)}, u32[]{:S(2)}, u32[]{:S(2)}) collective-permute-start(bf16[2,3,128,1024]{3,2,1,0:T(8,128)(2,1)} %collective-permute-done.20.refs_1_), channel_id=1, source_target_pairs={{0,8},{8,0},{1,9},{9,1},{2,10},{10,2},{3,11},{11,3},{4,12},{12,4},... | collective-permute-start | bytes 4718600 | tf_op jit(solution)/shard_map/ppermute | solution.py:167
  305.0 166.2 %collective-permute-start.25 = (bf16[2,3,128,1024]{3,2,1,0:T(8,128)(2,1)}, bf16[2,3,128,1024]{3,2,1,0:T(8,128)(2,1)}, u32[]{:S(2)}, u32[]{:S(2)}) collective-permute-start(bf16[2,3,128,1024]{3,2,1,0:T(8,128)(2,1)} %collective-permute-done.21.refs_2_), channel_id=1, source_target_pairs={{0,8},{8,0},{1,9},{9,1},{2,10},{10,2},{3,11},{11,3},{4,12},{12,4},... | collective-permute-start | bytes 4718600 | tf_op jit(solution)/shard_map/ppermute | solution.py:167
  336.0 135.2 %collective-permute-start.26 = (bf16[2,3,128,1024]{3,2,1,0:T(8,128)(2,1)}, bf16[2,3,128,1024]{3,2,1,0:T(8,128)(2,1)}, u32[]{:S(2)}, u32[]{:S(2)}) collective-permute-start(bf16[2,3,128,1024]{3,2,1,0:T(8,128)(2,1)} %collective-permute-done.22.refs_3_), channel_id=1, source_target_pairs={{0,8},{8,0},{1,9},{9,1},{2,10},{10,2},{3,11},{11,3},{4,12},{12,4},... | collective-permute-start | bytes 4718600 | tf_op jit(solution)/shard_map/ppermute | solution.py:167
  367.5 54.2 %collective-permute-start.18 = (bf16[2,48,2048]{2,1,0:T(8,128)(2,1)}, bf16[2,48,2048]{2,1,0:T(8,128)(2,1)}, u32[]{:S(2)}, u32[]{:S(2)}) collective-permute-start(bf16[2,48,2048]{2,1,0:T(8,128)(2,1)} %pad_maximum_fusion.9.refs_0_), channel_id=1, source_target_pairs={{0,1},{1,2},{2,3},{3,0},{4,5},{5,6},{6,7},{7,4},{8,9},{9,10},{10,1... | collective-permute-start | bytes 1179656 | tf_op jit(solution)/shard_map/ppermute | solution.py:134
  895.9 46.4 %collective-permute-start.57 = (bf16[4,48,2048]{2,1,0:T(8,128)(2,1)}, bf16[4,48,2048]{2,1,0:T(8,128)(2,1)}, u32[]{:S(2)}, u32[]{:S(2)}) collective-permute-start(bf16[4,48,2048]{2,1,0:T(8,128)(2,1)} %dynamic-slice_bitcast_fusion.3), channel_id=1, source_target_pairs={{0,4},{4,0},{1,5},{5,1},{2,6},{6,2},{3,7},{7,3},{8,12},{12,8},{9,1... | collective-permute-start | bytes 2359304 | tf_op jit(solution)/shard_map/ppermute | solution.py:156
  1015.1 121.1 %collective-permute-start.62 = (bf16[2,48,2048]{2,1,0:T(8,128)(2,1)S(1)}, bf16[2,48,2048]{2,1,0:T(8,128)(2,1)S(1)}, u32[]{:S(2)}, u32[]{:S(2)}) collective-permute-start(bf16[2,48,2048]{2,1,0:T(8,128)(2,1)S(1)} %pad_maximum_fusion.11.refs_0_), channel_id=1, source_target_pairs={{0,3},{1,0},{2,1},{3,2},{4,7},{5,4},{6,5},{7,6},{8,11},{9,8},{10,9... | collective-permute-start | bytes 1179656 | tf_op jit(solution)/shard_map/ppermute | solution.py:134
  1019.3 119.8 %collective-permute-start.63 = (bf16[2,48,2048]{2,1,0:T(8,128)(2,1)S(1)}, bf16[2,48,2048]{2,1,0:T(8,128)(2,1)}, u32[]{:S(2)}, u32[]{:S(2)}) collective-permute-start(bf16[2,48,2048]{2,1,0:T(8,128)(2,1)S(1)} %pad_maximum_fusion.11.refs_0_), channel_id=1, source_target_pairs={{0,2},{1,3},{2,0},{3,1},{4,6},{5,7},{6,4},{7,5},{8,10},{9,11},{10,... | collective-permute-start | bytes 1179656 | tf_op jit(solution)/shard_map/ppermute | solution.py:134
  1023.5 115.9 %collective-permute-start.64 = (bf16[2,48,2048]{2,1,0:T(8,128)(2,1)S(1)}, bf16[2,48,2048]{2,1,0:T(8,128)(2,1)}, u32[]{:S(2)}, u32[]{:S(2)}) collective-permute-start(bf16[2,48,2048]{2,1,0:T(8,128)(2,1)S(1)} %pad_maximum_fusion.11.refs_0_), channel_id=1, source_target_pairs={{0,1},{1,2},{2,3},{3,0},{4,5},{5,6},{6,7},{7,4},{8,9},{9,10},{10,1... | collective-permute-start | bytes 1179656 | tf_op jit(solution)/shard_map/ppermute | solution.py:134
  1027.7 55.7 %collective-permute-start.55 = (bf16[48,2048]{1,0:T(8,128)(2,1)}, bf16[48,2048]{1,0:T(8,128)(2,1)}, u32[]{:S(2)}, u32[]{:S(2)}) collective-permute-start(bf16[48,2048]{1,0:T(8,128)(2,1)} %copy-done.117), channel_id=1, source_target_pairs={{0,4},{4,0},{1,5},{5,1},{2,6},{6,2},{3,7},{7,3},{8,12},{12,8},{9,1... | collective-permute-start | bytes 589832 | tf_op jit(solution)/shard_map/ppermute | solution.py:138
  1031.3 52.2 %collective-permute-start.56 = (bf16[48,2048]{1,0:T(8,128)(2,1)}, bf16[48,2048]{1,0:T(8,128)(2,1)}, u32[]{:S(2)}, u32[]{:S(2)}) collective-permute-start(bf16[48,2048]{1,0:T(8,128)(2,1)} %copy-done.118), channel_id=1, source_target_pairs={{0,4},{4,0},{1,5},{5,1},{2,6},{6,2},{3,7},{7,3},{8,12},{12,8},{9,1... | collective-permute-start | bytes 589832 | tf_op jit(solution)/shard_map/ppermute | solution.py:138
  1083.4 300.2 %collective-permute-start.107 = (bf16[4,2,128,1024]{3,2,1,0:T(8,128)(2,1)}, bf16[4,2,128,1024]{3,2,1,0:T(8,128)(2,1)}, u32[]{:S(2)}, u32[]{:S(2)}) collective-permute-start(bf16[4,2,128,1024]{3,2,1,0:T(8,128)(2,1)} %dynamic-slice_bitcast_fusion), channel_id=1, source_target_pairs={{0,8},{8,0},{1,9},{9,1},{2,10},{10,2},{3,11},{11,3},{4,12},{12,4},... | collective-permute-start | bytes 6291464 | tf_op jit(solution)/shard_map/ppermute | solution.py:172
  1083.6 292.1 %collective-permute-start.102 = (bf16[4,2,128,1024]{3,2,1,0:T(8,128)(2,1)}, bf16[4,2,128,1024]{3,2,1,0:T(8,128)(2,1)}, u32[]{:S(2)}, u32[]{:S(2)}) collective-permute-start(bf16[4,2,128,1024]{3,2,1,0:T(8,128)(2,1)} %dynamic-slice_bitcast_fusion.1), channel_id=1, source_target_pairs={{0,8},{8,0},{1,9},{9,1},{2,10},{10,2},{3,11},{11,3},{4,12},{12,4},... | collective-permute-start | bytes 6291464 | tf_op jit(solution)/shard_map/ppermute | solution.py:172
  1136.2 179.8 %collective-permute-start.32 = (bf16[2,48,2048]{2,1,0:T(8,128)(2,1)}, bf16[2,48,2048]{2,1,0:T(8,128)(2,1)}, u32[]{:S(2)}, u32[]{:S(2)}) collective-permute-start(bf16[2,48,2048]{2,1,0:T(8,128)(2,1)} %pad_maximum_fusion.10.refs_0_), channel_id=1, source_target_pairs={{0,3},{1,0},{2,1},{3,2},{4,7},{5,4},{6,5},{7,6},{8,11},{9,8},{10,9... | collective-permute-start | bytes 1179656 | tf_op jit(solution)/shard_map/ppermute | solution.py:134
  1139.1 177.1 %collective-permute-start.33 = (bf16[2,48,2048]{2,1,0:T(8,128)(2,1)}, bf16[2,48,2048]{2,1,0:T(8,128)(2,1)}, u32[]{:S(2)}, u32[]{:S(2)}) collective-permute-start(bf16[2,48,2048]{2,1,0:T(8,128)(2,1)} %pad_maximum_fusion.10.refs_0_), channel_id=1, source_target_pairs={{0,2},{1,3},{2,0},{3,1},{4,6},{5,7},{6,4},{7,5},{8,10},{9,11},{10,... | collective-permute-start | bytes 1179656 | tf_op jit(solution)/shard_map/ppermute | solution.py:134
  1139.5 177.3 %collective-permute-start.34 = (bf16[2,48,2048]{2,1,0:T(8,128)(2,1)}, bf16[2,48,2048]{2,1,0:T(8,128)(2,1)}, u32[]{:S(2)}, u32[]{:S(2)}) collective-permute-start(bf16[2,48,2048]{2,1,0:T(8,128)(2,1)} %pad_maximum_fusion.10.refs_0_), channel_id=1, source_target_pairs={{0,1},{1,2},{2,3},{3,0},{4,5},{5,6},{6,7},{7,4},{8,9},{9,10},{10,1... | collective-permute-start | bytes 1179656 | tf_op jit(solution)/shard_map/ppermute | solution.py:134
  1316.1 74.9 %collective-permute-start.112 = (bf16[4,2,128,1024]{3,2,1,0:T(8,128)(2,1)}, bf16[4,2,128,1024]{3,2,1,0:T(8,128)(2,1)}, u32[]{:S(2)}, u32[]{:S(2)}) collective-permute-start(bf16[4,2,128,1024]{3,2,1,0:T(8,128)(2,1)} %bitcast.744), channel_id=1, source_target_pairs={{0,8},{8,0},{1,9},{9,1},{2,10},{10,2},{3,11},{11,3},{4,12},{12,4},... | collective-permute-start | bytes 6291464 | tf_op jit(solution)/shard_map/ppermute | solution.py:172
  1316.2 57.1 %collective-permute-start.76 = (bf16[2,768,128]{2,1,0:T(8,128)(2,1)S(1)}, bf16[2,768,128]{2,1,0:T(8,128)(2,1)S(1)}, u32[]{:S(2)}, u32[]{:S(2)}) collective-permute-start(bf16[2,768,128]{2,1,0:T(8,128)(2,1)S(1)} %fusion.116), channel_id=1, source_target_pairs={{0,8},{8,0},{1,9},{9,1},{2,10},{10,2},{3,11},{11,3},{4,12},{12,4},... | collective-permute-start | bytes 1179656 | tf_op jit(solution)/shard_map/ppermute | solution.py:199
  1381.6 65.7 %collective-permute-start.103 = (bf16[2,128,1024]{2,1,0:T(8,128)(2,1)}, bf16[2,128,1024]{2,1,0:T(8,128)(2,1)}, u32[]{:S(2)}, u32[]{:S(2)}) collective-permute-start(bf16[2,128,1024]{2,1,0:T(8,128)(2,1)} %get-tuple-element.561), channel_id=1, source_target_pairs={{0,32},{32,64},{64,96},{96,0},{1,33},{33,65},{65,97},{97,1},{2,34}... | collective-permute-start | bytes 1572872 | tf_op jit(solution)/shard_map/ppermute | solution.py:177
  1381.6 70.1 %collective-permute-start.104 = (bf16[2,128,1024]{2,1,0:T(8,128)(2,1)}, bf16[2,128,1024]{2,1,0:T(8,128)(2,1)}, u32[]{:S(2)}, u32[]{:S(2)}) collective-permute-start(bf16[2,128,1024]{2,1,0:T(8,128)(2,1)} %get-tuple-element.563), channel_id=1, source_target_pairs={{0,64},{32,96},{64,0},{96,32},{1,65},{33,97},{65,1},{97,33},{2,66}... | collective-permute-start | bytes 1572872 | tf_op jit(solution)/shard_map/ppermute | solution.py:177
  1383.7 68.1 %collective-permute-start.105 = (bf16[2,128,1024]{2,1,0:T(8,128)(2,1)}, bf16[2,128,1024]{2,1,0:T(8,128)(2,1)}, u32[]{:S(2)}, u32[]{:S(2)}) collective-permute-start(bf16[2,128,1024]{2,1,0:T(8,128)(2,1)} %get-tuple-element.562), channel_id=1, source_target_pairs={{0,96},{32,0},{64,32},{96,64},{1,97},{33,1},{65,33},{97,65},{2,98}... | collective-permute-start | bytes 1572872 | tf_op jit(solution)/shard_map/ppermute | solution.py:177
  1462.2 82.4 %collective-permute-start.97 = (bf16[4,2,128,640]{3,2,1,0:T(8,128)(2,1)}, bf16[4,2,128,640]{3,2,1,0:T(8,128)(2,1)}, u32[]{:S(2)}, u32[]{:S(2)}) collective-permute-start(bf16[4,2,128,640]{3,2,1,0:T(8,128)(2,1)} %bitcast.173), channel_id=1, source_target_pairs={{0,8},{8,0},{1,9},{9,1},{2,10},{10,2},{3,11},{11,3},{4,12},{12,4},... | collective-permute-start | bytes 3932168 | tf_op jit(solution)/shard_map/ppermute | solution.py:172
  1473.0 40.8 %collective-permute-start.78 = (bf16[4,48,2048]{2,1,0:T(8,128)(2,1)}, bf16[4,48,2048]{2,1,0:T(8,128)(2,1)}, u32[]{:S(2)}, u32[]{:S(2)}) collective-permute-start(bf16[4,48,2048]{2,1,0:T(8,128)(2,1)} %dynamic-slice_bitcast_fusion.2), channel_id=1, source_target_pairs={{0,4},{4,0},{1,5},{5,1},{2,6},{6,2},{3,7},{7,3},{8,12},{12,8},{9,1... | collective-permute-start | bytes 2359304 | tf_op jit(solution)/shard_map/ppermute | solution.py:156
  1475.5 46.2 %collective-permute-start.89 = (bf16[48,2048]{1,0:T(8,128)(2,1)}, bf16[48,2048]{1,0:T(8,128)(2,1)}, u32[]{:S(2)}, u32[]{:S(2)}) collective-permute-start(bf16[48,2048]{1,0:T(8,128)(2,1)} %fusion.117), channel_id=1, source_target_pairs={{0,4},{4,0},{1,5},{5,1},{2,6},{6,2},{3,7},{7,3},{8,12},{12,8},{9,1... | collective-permute-start | bytes 589832 | tf_op jit(solution)/shard_map/ppermute | solution.py:155
  1549.2 68.6 %collective-permute-start.84 = (bf16[2,48,2048]{2,1,0:T(8,128)(2,1)S(1)}, bf16[2,48,2048]{2,1,0:T(8,128)(2,1)}, u32[]{:S(2)}, u32[]{:S(2)}) collective-permute-start(bf16[2,48,2048]{2,1,0:T(8,128)(2,1)S(1)} %pad_maximum_fusion.13.refs_0_), channel_id=1, source_target_pairs={{0,2},{1,3},{2,0},{3,1},{4,6},{5,7},{6,4},{7,5},{8,10},{9,11},{10,... | collective-permute-start | bytes 1179656 | tf_op jit(solution)/shard_map/ppermute | solution.py:134
  1551.0 66.8 %collective-permute-start.85 = (bf16[2,48,2048]{2,1,0:T(8,128)(2,1)S(1)}, bf16[2,48,2048]{2,1,0:T(8,128)(2,1)}, u32[]{:S(2)}, u32[]{:S(2)}) collective-permute-start(bf16[2,48,2048]{2,1,0:T(8,128)(2,1)S(1)} %pad_maximum_fusion.13.refs_0_), channel_id=1, source_target_pairs={{0,1},{1,2},{2,3},{3,0},{4,5},{5,6},{6,7},{7,4},{8,9},{9,10},{10,1... | collective-permute-start | bytes 1179656 | tf_op jit(solution)/shard_map/ppermute | solution.py:134
  1552.4 115.0 %collective-permute-start.100 = (bf16[2,128,640]{2,1,0:T(8,128)(2,1)}, bf16[2,128,640]{2,1,0:T(8,128)(2,1)}, u32[]{:S(2)}, u32[]{:S(2)}) collective-permute-start(bf16[2,128,640]{2,1,0:T(8,128)(2,1)} %get-tuple-element.578), channel_id=1, source_target_pairs={{0,96},{32,0},{64,32},{96,64},{1,97},{33,1},{65,33},{97,65},{2,98}... | collective-permute-start | bytes 983048 | tf_op jit(solution)/shard_map/ppermute | solution.py:177
  1562.1 105.3 %collective-permute-start.98 = (bf16[2,128,640]{2,1,0:T(8,128)(2,1)}, bf16[2,128,640]{2,1,0:T(8,128)(2,1)}, u32[]{:S(2)}, u32[]{:S(2)}) collective-permute-start(bf16[2,128,640]{2,1,0:T(8,128)(2,1)} %get-tuple-element.577), channel_id=1, source_target_pairs={{0,32},{32,64},{64,96},{96,0},{1,33},{33,65},{65,97},{97,1},{2,34}... | collective-permute-start | bytes 983048 | tf_op jit(solution)/shard_map/ppermute | solution.py:177
  1563.0 104.4 %collective-permute-start.99 = (bf16[2,128,640]{2,1,0:T(8,128)(2,1)}, bf16[2,128,640]{2,1,0:T(8,128)(2,1)}, u32[]{:S(2)}, u32[]{:S(2)}) collective-permute-start(bf16[2,128,640]{2,1,0:T(8,128)(2,1)} %get-tuple-element.579), channel_id=1, source_target_pairs={{0,64},{32,96},{64,0},{96,32},{1,65},{33,97},{65,1},{97,33},{2,66}... | collective-permute-start | bytes 983048 | tf_op jit(solution)/shard_map/ppermute | solution.py:177
  (272 other events, 4803.6 us)

commit v2 on v1

--- a/solution.py
+++ b/solution.py
@@ -24,6 +24,10 @@
 
 F32 = jnp.float32
 BF16 = jnp.bfloat16
+QB = 128
+KB = 512
+
+
 SWAP = ((0, 1), (1, 0))
 
 
@@ -31,36 +35,273 @@
     return tuple((i, (i + step) % 4) for i in range(4))
 
 
-def layout_slots(lengths, groups, group_id, slot_ids):
+def dot(a, b):
+    return jnp.dot(a, b, preferred_element_type=F32)
+
+
+def turn(value, cosine, sine):
+    a, b = value[: HD // 2], value[HD // 2 :]
+    return jnp.concatenate([a * cosine - b * sine, b * cosine + a * sine], axis=0)
+
+
+def heads_to_lanes(wide, heads):
+    return jnp.concatenate([wide[h * HD : (h + 1) * HD] for h in range(heads)], axis=1)
+
+
+def lanes_to_heads(tall, heads):
+    n = tall.shape[1] // heads
+    return jnp.concatenate([tall[:, h * n : (h + 1) * n] for h in range(heads)], axis=0)
+
+
+def normed_projections(tokens, gain, w_query, w_kv, cosine, sine, eps):
+    rows, width = tokens.shape
+    block = 256
+
+    def kernel(t_ref, g_ref, wq_ref, wkv_ref, cos_ref, sin_ref, n_ref, q_ref, kv_ref):
+        x = t_ref[...].astype(F32)
+        inv = lax.rsqrt(jnp.mean(x * x, axis=-1, keepdims=True) + eps)
+        normed = (x * inv * g_ref[...].astype(F32)).astype(BF16)
+        n_ref[...] = normed
+        q_ref[...] = dot(normed, wq_ref[...])
+        kv = jnp.transpose(dot(normed, wkv_ref[...]))
+        kv = jnp.concatenate([turn(kv[:HD], cos_ref[...], sin_ref[...]), kv[HD:]], axis=0)
+        kv_ref[...] = jnp.transpose(kv).astype(BF16)
+
+    whole = lambda a: pl.BlockSpec(a.shape, lambda i: (0,) * a.ndim)
+    by_row = lambda w: pl.BlockSpec((block, w), lambda i: (i, 0))
+    by_lane = pl.BlockSpec((HD // 2, block), lambda i: (0, i))
+    return pl.pallas_call(
+        kernel,
+        grid=(rows // block,),
+        in_specs=[by_row(width), whole(gain), whole(w_query), whole(w_kv), by_lane, by_lane],
+        out_specs=[by_row(width), by_row(w_query.shape[1]), by_row(2 * HD)],
+        out_shape=[
+            jax.ShapeDtypeStruct((rows, width), BF16),
+            jax.ShapeDtypeStruct((rows, w_query.shape[1]), F32),
+            jax.ShapeDtypeStruct((rows, 2 * HD), BF16),
+        ],
+        cost_estimate=pl.CostEstimate(
+            flops=rows * width * 384, bytes_accessed=4 << 20, transcendentals=0
+        ),
+        compiler_params=pltpu.CompilerParams(vmem_limit_bytes=32 << 20),
+    )(tokens, gain, w_query, w_kv, cosine, sine)
+
+
+def key_ranges(bounds_ref, step):
+    return [bounds_ref[step * 4 + n] for n in range(4)]
+
+
+def attention_forward(query_raw, kv, bounds, starts, slots, cosine, sine, row_offset, rows):
+    heads = query_raw.shape[1] // HD
+    keys = kv.shape[0]
+    wide = heads * QB
+    steps, base = rows // QB, row_offset // QB
+
+    def kernel(b_ref, q_ref, kv_ref, start_ref, slot_ref, cos_ref, sin_ref, m_ref, qt_ref, ot_ref, lse_ref, kvt_ref, qp_ref):
+        step = pl.program_id(0)
+
+        @pl.when(step == 0)
+        def _():
+            kvt_ref[...] = jnp.transpose(kv_ref[...].astype(F32)).astype(BF16)
+
+        raw = jnp.transpose(q_ref[...])
+        turned = jnp.concatenate(
+            [turn(raw[h * HD : (h + 1) * HD], cos_ref[...], sin_ref[...]) for h in range(heads)],
+            axis=1,
+        ).astype(BF16)
+        qt_ref[0] = turned
+        scaled = (turned.astype(F32) * HD**-0.5).astype(BF16)
+        qp_ref[...] = jnp.concatenate([scaled, jnp.zeros_like(scaled)], axis=0)
+        start = jnp.concatenate([start_ref[0]] * heads, axis=1)
+        slot = jnp.concatenate([slot_ref[0]] * heads, axis=1)
+
+        def body(masked, j, carry):
+            peak, total, acc = carry
+            at = pl.multiple_of(j * KB, KB)
+            scores = dot(kv_ref[pl.ds(at, KB), :], qp_ref[...])
+            if masked:
+                key = at + lax.broadcasted_iota(jnp.int32, (KB, wide), 0)
+                scores = jnp.where((key >= start) & (key <= slot), scores, MASKED_SCORE)
+            new_peak = jnp.maximum(peak, jnp.max(scores, axis=0, keepdims=True))
+            powers = jnp.exp(scores - new_peak)
+            shrink = jnp.exp(peak - new_peak)
+            total = total * shrink + jnp.sum(powers, axis=0, keepdims=True)
+            values = kvt_ref[HD:, pl.ds(at, KB)]
+            acc = acc * shrink + dot(values, powers.astype(BF16))
+            return (new_peak, total, acc)
+
+        first, full_first, full_end, end = key_ranges(b_ref, base + step)
+        carry = (
+            jnp.full((1, wide), MASKED_SCORE, F32),
+            jnp.zeros((1, wide), F32),
+            jnp.zeros((HD, wide), F32),
+        )
+        carry = lax.fori_loop(first, full_first, functools.partial(body, True), carry)
+        carry = lax.fori_loop(full_first, full_end, functools.partial(body, False), carry)
+        carry = lax.fori_loop(full_end, end, functools.partial(body, True), carry)
+        peak, total, acc = carry
+        mixed = acc / total
+        ot_ref[0] = mixed
+        lse_ref[0] = peak + jnp.log(total)
+        m_ref[...] = jnp.transpose(lanes_to_heads(mixed, heads)).astype(BF16)
+
+    lane = lambda: pl.BlockSpec((HD // 2, QB), lambda i: (0, base + i))
+    row = lambda: pl.BlockSpec((1, 1, QB), lambda i: (base + i, 0, 0))
+    return pl.pallas_call(
+        kernel,
+        grid=(steps,),
+        in_specs=[
+            pl.BlockSpec(memory_space=pltpu.SMEM),
+            pl.BlockSpec((QB, heads * HD), lambda i: (base + i, 0)),
+            pl.BlockSpec((keys, 2 * HD), lambda i: (0, 0)),
+            row(),
+            row(),
+            lane(),
+            lane(),
+        ],
+        out_specs=[
+            pl.BlockSpec((QB, heads * HD), lambda i: (i, 0)),
+            pl.BlockSpec((1, HD, wide), lambda i: (i, 0, 0)),
+            pl.BlockSpec((1, HD, wide), lambda i: (i, 0, 0)),
+            pl.BlockSpec((1, 1, wide), lambda i: (i, 0, 0)),
+        ],
+        out_shape=[
+            jax.ShapeDtypeStruct((rows, heads * HD), BF16),
+            jax.ShapeDtypeStruct((steps, HD, wide), BF16),
+            jax.ShapeDtypeStruct((steps, HD, wide), F32),
+            jax.ShapeDtypeStruct((steps, 1, wide), F32),
+        ],
+        scratch_shapes=[pltpu.VMEM((2 * HD, keys), BF16), pltpu.VMEM((2 * HD, wide), BF16)],
+        cost_estimate=pl.CostEstimate(
+            flops=rows * 2 * keys * heads * HD, bytes_accessed=2 << 20, transcendentals=0
+        ),
+        compiler_params=pltpu.CompilerParams(vmem_limit_bytes=32 << 20),
+    )(bounds, query_raw, kv, starts, slots, cosine, sine)
+
+
+def attention_backward(d_mixed, kv, queries, mixed, lse, bounds, starts, slots, cosine, sine):
+    rows, width = d_mixed.shape
+    heads = width // HD
+    keys = kv.shape[0]
+    wide = heads * QB
+    steps = rows // QB
+
+    def kernel(b_ref, d_ref, kv_ref, qt_ref, ot_ref, lse_ref, start_ref, slot_ref, cos_ref, sin_ref, dq_ref, dkv_ref, kvt_ref, qp_ref, dp_ref, qr_ref, dr_ref):
+        step = pl.program_id(0)
+
+        @pl.when(step == 0)
+        def _():
+            kvt_ref[...] = jnp.transpose(kv_ref[...].astype(F32)).astype(BF16)
+            dkv_ref[...] = jnp.zeros_like(dkv_ref)
+
+        scaled = qt_ref[0].astype(F32) * HD**-0.5
+        grads = heads_to_lanes(jnp.transpose(d_ref[...].astype(F32)), heads)
+        delta = jnp.sum(grads * ot_ref[0], axis=0, keepdims=True)
+        empty = jnp.zeros_like(scaled)
+        q_pad = jnp.concatenate([scaled, empty], axis=0)
+        d_pad = jnp.concatenate([empty, grads], axis=0)
+        qp_ref[...] = q_pad.astype(BF16)
+        dp_ref[...] = d_pad.astype(BF16)
+        qr_ref[...] = jnp.transpose(q_pad).astype(BF16)
+        dr_ref[...] = jnp.transpose(d_pad).astype(BF16)
+        start = jnp.concatenate([start_ref[0]] * heads, axis=1)
+        slot = jnp.concatenate([slot_ref[0]] * heads, axis=1)
+        log_total = lse_ref[0]
+
+        def body(masked, j, d_query):
+            at = pl.multiple_of(j * KB, KB)
+            block = kv_ref[pl.ds(at, KB), :]
+            scores = dot(block, qp_ref[...])
+            if masked:
+                key = at + lax.broadcasted_iota(jnp.int32, (KB, wide), 0)
+                scores = jnp.where((key >= start) & (key <= slot), scores, MASKED_SCORE)
+            chances = jnp.exp(scores - log_total)
+            d_chances = dot(block, dp_ref[...])
+            d_scores = (chances * (d_chances - delta)).astype(BF16)
+            dkv_ref[pl.ds(at, KB), :] += dot(chances.astype(BF16), dr_ref[...]) + dot(
+                d_scores, qr_ref[...]
+            )
+            return d_query + dot(kvt_ref[:HD, pl.ds(at, KB)], d_scores)
+
+        first, full_first, full_end, end = key_ranges(b_ref, step)
+        d_query = jnp.zeros((HD, wide), F32)
+        d_query = lax.fori_loop(first, full_first, functools.partial(body, True), d_query)
+        d_query = lax.fori_loop(full_first, full_end, functools.partial(body, False), d_query)
+        d_query = lax.fori_loop(full_end, end, functools.partial(body, True), d_query)
+        d_query = lanes_to_heads(d_query * HD**-0.5, heads)
+        turned = jnp.concatenate(
+            [turn(d_query[h * HD : (h + 1) * HD], cos_ref[...], -sin_ref[...]) for h in range(heads)],
+            axis=0,
+        )
+        dq_ref[...] = jnp.transpose(turned).astype(BF16)
+
+    lane = lambda: pl.BlockSpec((HD // 2, QB), lambda i: (0, i))
+    row = lambda: pl.BlockSpec((1, 1, QB), lambda i: (i, 0, 0))
+    kept = lambda n: pl.BlockSpec((1, n, wide), lambda i: (i, 0, 0))
+    return pl.pallas_call(
+        kernel,
+        grid=(steps,),
+        in_specs=[
+            pl.BlockSpec(memory_space=pltpu.SMEM),
+            pl.BlockSpec((QB, width), lambda i: (i, 0)),
+            pl.BlockSpec((keys, 2 * HD), lambda i: (0, 0)),
+            kept(HD),
+            kept(HD),
+            kept(1),
+            row(),
+            row(),
+            lane(),
+            lane(),
+        ],
+        out_specs=[
+            pl.BlockSpec((QB, width), lambda i: (i, 0)),
+            pl.BlockSpec((keys, 2 * HD), lambda i: (0, 0)),
+        ],
+        out_shape=[
+            jax.ShapeDtypeStruct((rows, width), BF16),
+            jax.ShapeDtypeStruct((keys, 2 * HD), F32),
+        ],
+        scratch_shapes=[
+            pltpu.VMEM((2 * HD, keys), BF16),
+            pltpu.VMEM((2 * HD, wide), BF16),
+            pltpu.VMEM((2 * HD, wide), BF16),
+            pltpu.VMEM((wide, 2 * HD), BF16),
+            pltpu.VMEM((wide, 2 * HD), BF16),
+        ],
+        cost_estimate=pl.CostEstimate(
+            flops=rows * 4 * keys * heads * HD, bytes_accessed=2 << 20, transcendentals=0
+        ),
+        compiler_params=pltpu.CompilerParams(vmem_limit_bytes=32 << 20),
+    )(bounds, d_mixed, kv, queries, mixed, lse, starts, slots, cosine, sine)
+
+
+def slot_tables(lengths, groups, group_id, first_slot, rows):
     seq_count = lengths.shape[0]
     seq_order = jnp.arange(seq_count, dtype=jnp.int32)
     same_group = groups[None, :] == groups[:, None]
     before = seq_order[None, :] < seq_order[:, None]
-    starts = jnp.sum(jnp.where(same_group & before, lengths[None, :], 0), axis=1)
-    ends = starts + lengths
+    begins = jnp.sum(jnp.where(same_group & before, lengths[None, :], 0), axis=1)
+    ends = begins + lengths
+    slots = first_slot + jnp.arange(rows, dtype=jnp.int32)
     inside = (
         (groups == group_id)[:, None]
-        & (slot_ids[None, :] >= starts[:, None])
-        & (slot_ids[None, :] < ends[:, None])
-    )
-    document = jnp.sum(jnp.where(inside, seq_order[:, None] + 1, 0), axis=0) - 1
-    position = jnp.sum(jnp.where(inside, slot_ids[None, :] - starts[:, None], 0), axis=0)
-    document = jnp.where(document < 0, seq_count + slot_ids, document)
-    return (document, position)
-
-
-def rotate(values, position, direction):
-    half_dim = values.shape[-1] // 2
-    frequency = ROPE_BASE ** (-2.0 * jnp.arange(half_dim, dtype=jnp.float32) / values.shape[-1])
-    angles = position.astype(jnp.float32)[:, None] * frequency[None, :]
-    cosine = jnp.cos(angles)[:, None, :]
-    sine_part = direction * jnp.sin(angles)[:, None, :]
-    first_half = values[..., :half_dim]
-    second = values[..., half_dim:]
-    return jnp.concatenate(
-        [first_half * cosine - second * sine_part, second * cosine + first_half * sine_part],
-        axis=-1,
-    )
+        & (slots[None, :] >= begins[:, None])
+        & (slots[None, :] < ends[:, None])
+    )
+    starts = jnp.where(
+        jnp.any(inside, axis=0), jnp.sum(jnp.where(inside, begins[:, None], 0), axis=0), slots
+    )
+    return slots, starts
+
+
+def block_bounds(slots, starts):
+    first_row, last_row = slots[::QB], slots[QB - 1 :: QB]
+    low, high = starts[::QB], starts[QB - 1 :: QB]
+    first = low // KB
+    end = last_row // KB + 1
+    full_first = jnp.clip((high + KB - 1) // KB, first, end)
+    full_end = jnp.clip((first_row + 1) // KB, full_first, end)
+    return jnp.stack([first, full_first, full_end, end], axis=1).reshape(-1).astype(jnp.int32)
 
 
 def adamw_step(weight, first, second, grad, rate, decay):
@@ -77,29 +318,125 @@
     size = sum(p.size * p.dtype.itemsize for p in pieces)
 
     def kernel(table_ref, *refs):
-        sources, outs, sem = refs[: len(pieces)], refs[len(pieces) : -1], refs[-1]
-        copies = []
-        for n, (piece, source_index, out, entry) in enumerate(plan):
-            source = sources[piece]
-            if source_index is not None:
-                source = source.at[source_index]
-            copies.append(
-                pltpu.make_async_copy(source, outs[out].at[table_ref[entry]], sem.at[n])
-            )
-        for copy in copies:
-            copy.start()
-        for copy in copies:
-            copy.wait()
+        count = len(pieces)
+        sources, refs = refs[:count], refs[count:]
+        outs, refs = refs[: len(out_shapes)], refs[len(out_shapes) :]
+        held, into, back = refs[:count], refs[count], refs[count + 1]
+        loads = [
+            pltpu.make_async_copy(sources[i], held[i], into.at[i]) for i in range(count)
+        ]
+        for load in loads:
+            load.start()
+        stores = []
+        for i in range(count):
+            loads[i].wait()
+            for piece, source_index, out, entry in plan:
+                if piece != i:
+                    continue
+                source = held[i] if source_index is None else held[i].at[source_index]
+                store = pltpu.make_async_copy(
+                    source, outs[out].at[table_ref[entry]], back.at[len(stores)]
+                )
+                store.start()
+                stores.append(store)
+        for store in stores:
+            store.wait()
 
     return pl.pallas_call(
         kernel,
         out_shape=[jax.ShapeDtypeStruct(s, BF16) for s in out_shapes],
         in_specs=[pl.BlockSpec(memory_space=pltpu.SMEM)]
-        + [pl.BlockSpec(memory_space=pl.ANY)] * len(pieces),
-        out_specs=[pl.BlockSpec(memory_space=pl.ANY)] * len(out_shapes),
-        scratch_shapes=[pltpu.SemaphoreType.DMA((moves,))],
+        + [pl.BlockSpec(memory_space=pltpu.HBM)] * len(pieces),
+        out_specs=[pl.BlockSpec(memory_space=pltpu.HBM)] * len(out_shapes),
+        scratch_shapes=[pltpu.VMEM(p.shape, p.dtype) for p in pieces]
+        + [pltpu.SemaphoreType.DMA((len(pieces),)), pltpu.SemaphoreType.DMA((moves,))],
         cost_estimate=pl.CostEstimate(flops=0, bytes_accessed=2 * size, transcendentals=0),
+        compiler_params=pltpu.CompilerParams(vmem_limit_bytes=size + (2 << 20)),
     )(table, *pieces)
+
+
+def outer_blocks(table, groups):
+    lefts, rights, plan = [], [], []
+    for pairs in groups:
+        entry = []
+        for left, right in pairs:
+            spot = next((n for n, known in enumerate(lefts) if known is left), None)
+            if spot is None:
+                spot = len(lefts)
+                lefts.append(left)
+            entry.append((spot, len(rights)))
+            rights.append(right)
+        plan.append(entry)
+    width = sum(pairs[0][1].shape[1] for pairs in groups)
+    block = D // 16
+
+    def kernel(table_ref, *refs):
+        left_refs, refs = refs[: len(lefts)], refs[len(lefts) :]
+        right_refs, (give_ref, keep_ref) = refs[: len(rights)], refs[len(rights) :]
+        step = pl.program_id(0)
+        turned = [jnp.transpose(r[...]) for r in left_refs]
+        parts = []
+        for entry in plan:
+            part = None
+            for spot, n in entry:
+                term = dot(turned[spot], right_refs[n][...])
+                part = term if part is None else part + term
+            parts.append(part.astype(BF16))
+        whole = parts[0] if len(parts) == 1 else jnp.concatenate(parts, axis=1)
+
+        @pl.when(step < 8)
+        def _():
+            give_ref[...] = whole
+
+        @pl.when(step >= 8)
+        def _():
+            keep_ref[...] = whole
+
+    flops = sum(2 * left.shape[0] * D * right.shape[1] for g in groups for left, right in g)
+    return pl.pallas_call(
+        kernel,
+        grid_spec=pltpu.PrefetchScalarGridSpec(
+            num_scalar_prefetch=1,
+            grid=(16,),
+            in_specs=[pl.BlockSpec((v.shape[0], block), lambda i, t: (0, t[i])) for v in lefts]
+            + [pl.BlockSpec(v.shape, lambda i, t: (0, 0)) for v in rights],
+            out_specs=[
+                pl.BlockSpec((block, width), lambda i, t: (jnp.minimum(i, 7), 0)),
+                pl.BlockSpec((block, width), lambda i, t: (jnp.maximum(i - 8, 0), 0)),
+            ],
+        ),
+        out_shape=[jax.ShapeDtypeStruct((8 * block, width), BF16)] * 2,
+        cost_estimate=pl.CostEstimate(flops=flops, bytes_accessed=4 << 20, transcendentals=0),
+        compiler_params=pltpu.CompilerParams(vmem_limit_bytes=32 << 20),
+    )(table, *lefts, *rights)
+
+
+def adamw_kernel(weight, first, second, keep, got, rate, flip):
+    def kernel(w_ref, m_ref, v_ref, keep_ref, got_ref, m_out, v_out, w_out, sum_ref):
+        grad = keep_ref[...] + got_ref[...].astype(F32)
+        if flip:
+            grad = jnp.transpose(grad)
+        weight = w_ref[...]
+        first_new, second_new, weight_new = adamw_step(
+            weight, m_ref[...], v_ref[...], grad, rate, DECAY_RATE
+        )
+        m_out[...] = first_new
+        v_out[...] = second_new
+        w_out[...] = weight_new
+        if flip:
+            sum_ref[...] = jnp.zeros_like(sum_ref)
+        else:
+            sum_ref[...] = jnp.sum(weight.astype(BF16).astype(F32) * grad, axis=1, keepdims=True)
+
+    shape = jax.ShapeDtypeStruct(weight.shape, F32)
+    return pl.pallas_call(
+        kernel,
+        out_shape=[shape] * 3 + [jax.ShapeDtypeStruct((D // 16, 1), F32)],
+        cost_estimate=pl.CostEstimate(
+            flops=0, bytes_accessed=28 * weight.size, transcendentals=0
+        ),
+        compiler_params=pltpu.CompilerParams(vmem_limit_bytes=16 << 20),
+    )(weight, first, second, keep, got)
 
 
 def pick(blocks, axis, index):
@@ -121,9 +458,9 @@
         table = []
         for dc in range(2):
             core = self.c if dc == 0 else 1 - self.c
-            for dy in range(2):
-                yh = self.yh if dy == 0 else 1 - self.yh
-                for k in range(4):
+            for k in range(4):
+                for dy in range(2):
+                    yh = self.yh if dy == 0 else 1 - self.yh
                     table.append(((self.x + k) % 4) * 4 + yh * 2 + core)
         return jnp.stack(table).astype(jnp.int32)
 
@@ -166,17 +503,15 @@
         mine = [pair] + [lax.ppermute(pair, "x", ring(-k)) for k in (1, 2, 3)]
         return mine + [lax.ppermute(p, "c", SWAP) for p in mine]
 
-    def scatter_weights(self, terms):
-        w = terms.shape[1]
-        blocks = terms.reshape(4, 2, 2, D // 16, w)
-        got = lax.ppermute(pick(blocks, 2, 1 - self.c), "c", SWAP)
-        both = pick(blocks, 2, self.c).astype(F32) + got.astype(F32)
-        low = both.astype(BF16)
-        total = pick(both, 0, self.x)
+    def scatter_weights(self, give, keep):
+        got = lax.ppermute(give, "c", SWAP)
+        n = D // 8
+        both = lambda k: keep[k * n : (k + 1) * n].astype(F32) + got[k * n : (k + 1) * n].astype(F32)
+        total = both(0)
         for k in (1, 2, 3):
-            total = total + lax.ppermute(pick(low, 0, (self.x + k) % 4), "x", ring(k)).astype(F32)
-        give = pick(total, 0, 1 - self.yh).astype(BF16)
-        return pick(total, 0, self.yh) + lax.ppermute(give, "yh", SWAP).astype(F32)
+            total = total + lax.ppermute(both(k).astype(BF16), "x", ring(k)).astype(F32)
+        back = lax.ppermute(total[n // 2 :].astype(BF16), "yh", SWAP)
+        return total[: n // 2], back
 
     def gather_ctx(self, own):
         over = lax.ppermute(own, "yh", SWAP)
@@ -244,7 +579,6 @@
     tp_id = here.yl * 4 + here.z
     half = row_count // 2
     part = half // 8
-    scale = HD ** (-0.5)
     ztable = here.ztable()
     xtable = here.xtable()
 
@@ -258,7 +592,7 @@
     plan = []
     for i in range(8):
         for d in range(2):
-            entry = (i // 4) * 8 + d * 4 + i % 4
+            entry = 2 * i + d
             rows = pl.ds(0, D // 16)
             plan.append((i, (d, rows, pl.ds(0, q_cols)), 0, entry))
             plan.append((i, (d, rows, pl.ds(q_cols, kv_cols)), 1, entry))
@@ -283,52 +617,33 @@
     for i in range(8):
         for d in range(2):
             for o in range(3):
-                plan.append((i, (d, o), o, (i // 4) * 8 + d * 4 + i % 4))
+                plan.append((i, (d, o), o, 2 * i + d))
     w_gate, w_up, w_down = (
         w.reshape(D, units) for w in place(ff_pieces, plan, xtable, [(16, D // 16, units)] * 3)
     )
 
-    key_doc, key_pos = layout_slots(
-        lengths, groups, group_id, jnp.arange(group_rows, dtype=jnp.int32)
-    )
-    own_doc, own_pos = layout_slots(
-        lengths, groups, group_id, ctx_id * row_count + jnp.arange(row_count, dtype=jnp.int32)
-    )
-    visible = (own_doc[:, None] == key_doc[None, :]) & (key_pos[None, :] <= own_pos[:, None])
-
-    inputs = tokens.astype(F32)
-    inv_one = lax.rsqrt(jnp.mean(inputs * inputs, axis=-1, keepdims=True) + NORM_EPS)
-    normed_one = (inputs * inv_one * gain_values[0]).astype(BF16)
-    head_count = q_cols // HD
-    kv_raw = jnp.dot(normed_one, w_kv, preferred_element_type=F32).reshape(row_count, 1, 2 * HD)
-    kv_local = jnp.concatenate(
-        [rotate(kv_raw[..., :HD], own_pos, 1.0), kv_raw[..., HD:]], axis=-1
-    ).astype(BF16)
-    kv_whole = here.gather_ctx(kv_local.reshape(row_count, 2 * HD))
-    key_head, value_head = kv_whole[:, :HD], kv_whole[:, HD:]
-    query_raw = jnp.dot(normed_one, w_query, preferred_element_type=F32).reshape(
-        row_count, head_count, HD
-    )
-    queries = rotate(query_raw, own_pos, 1.0).astype(BF16).transpose(1, 0, 2)
-
-    def forward_head(query_head):
-        scores = (
-            jnp.einsum("rd,kd->rk", query_head, key_head, preferred_element_type=F32) * scale
-        )
-        scores = jnp.where(visible, scores, MASKED_SCORE)
-        row_peak = jnp.max(scores, axis=-1, keepdims=True)
-        powers = jnp.exp(scores - row_peak)
-        summed = jnp.sum(powers, axis=-1, keepdims=True)
-        chances = (powers / summed).astype(BF16)
-        mixed_head = jnp.dot(chances, value_head, preferred_element_type=F32)
-        return (mixed_head, (row_peak + jnp.log(summed))[:, 0])
-
-    mixed_heads, log_totals = lax.map(forward_head, queries)
-    mixed = mixed_heads.transpose(1, 0, 2).reshape(row_count, head_count * HD).astype(BF16)
+    slots, starts = slot_tables(lengths, groups, group_id, ctx_id * row_count, row_count)
+    frequency = ROPE_BASE ** (-2.0 * jnp.arange(HD // 2, dtype=F32) / HD)
+    angles = frequency[:, None] * (slots - starts).astype(F32)[None, :]
+    cosine, sine = jnp.cos(angles), jnp.sin(angles)
+    bounds = block_bounds(slots, starts)
+    slot_rows, start_rows = slots.reshape(-1, 1, QB), starts.reshape(-1, 1, QB)
+
+    normed_one, query_raw, kv_local = normed_projections(
+        tokens, gain_values[:1].astype(BF16), w_query, w_kv, cosine, sine, NORM_EPS
+    )
+    kv_whole = here.gather_ctx(kv_local)
 
     halves = (0, 1)
     z_first = (False, True)
-    mixed_half = [mixed[:half], mixed[half:]]
+    mixed_half, turned_half, raw_half, total_half = zip(
+        *[
+            attention_forward(
+                query_raw, kv_whole, bounds, start_rows, slot_rows, cosine, sine, h * half, half
+            )
+            for h in halves
+        ]
+    )
     cotangent_half = [cotangent[:half], cotangent[half:]]
     own_start = [h * half + tp_id * part for h in halves]
     own_inputs = [
@@ -389,43 +704,29 @@
         outputs.append(here.gather_tp(own_out, z_first[h], ztable))
     output = jnp.concatenate(outputs)
 
-    both = lambda pair: jnp.concatenate(pair, axis=0)
-    normed_two_all = both(normed_two)
-    outer = lambda a, b: jnp.einsum("rd,rf->df", a, b, preferred_element_type=F32).astype(BF16)
-    grad_gate = here.scatter_weights(outer(normed_two_all, both(d_gate)))
-    grad_up = here.scatter_weights(outer(normed_two_all, both(d_up)))
-    grad_down = here.scatter_weights(outer(cotangent, both(hidden))).T
-
-    d_mixed = d_mixed.reshape(row_count, head_count, HD).transpose(1, 0, 2)
-
-    def backward_head(operands):
-        query_head, d_head, log_total = operands
-        scores = (
-            jnp.einsum("rd,kd->rk", query_head, key_head, preferred_element_type=F32) * scale
-        )
-        scores = jnp.where(visible, scores, MASKED_SCORE)
-        chances = jnp.exp(scores - log_total[:, None])
-        d_value = jnp.einsum("rk,rd->kd", chances.astype(BF16), d_head, preferred_element_type=F32)
-        d_chances = jnp.einsum("rd,kd->rk", d_head, value_head, preferred_element_type=F32)
-        centre = jnp.sum(chances * d_chances, axis=-1, keepdims=True)
-        d_scores = (chances * (d_chances - centre)).astype(BF16)
-        d_query = jnp.dot(d_scores, key_head, preferred_element_type=F32) * scale
-        d_key = jnp.einsum("rk,rd->kd", d_scores, query_head, preferred_element_type=F32) * scale
-        return (d_query, d_key, d_value)
-
-    d_queries, d_keys, d_values = lax.map(backward_head, (queries, d_mixed, log_totals))
-    d_kv = jnp.concatenate([d_keys.sum(axis=0), d_values.sum(axis=0)], axis=-1)
-    d_kv_own = here.scatter_ctx(d_kv)[:, None]
+    order = here.xtable()
+    order = jnp.concatenate([order[8:], order[:8]])
+    pairs = lambda lefts, rights: [tuple(zip(lefts, rights))]
+    gate_sum = here.scatter_weights(*outer_blocks(order, pairs(normed_two, d_gate)))
+    up_sum = here.scatter_weights(*outer_blocks(order, pairs(normed_two, d_up)))
+    down_sum = here.scatter_weights(*outer_blocks(order, pairs(cotangent_half, hidden)))
+
+    d_query_low, d_kv = attention_backward(
+        d_mixed,
+        kv_whole,
+        jnp.concatenate(turned_half),
+        jnp.concatenate(raw_half),
+        jnp.concatenate(total_half),
+        bounds,
+        start_rows,
+        slot_rows,
+        cosine,
+        sine,
+    )
+    d_kv_own = here.scatter_ctx(d_kv).T
     d_kv_low = (
-        jnp.concatenate([rotate(d_kv_own[..., :HD], own_pos, -1.0), d_kv_own[..., HD:]], axis=-1)
-        .astype(BF16)
-        .reshape(row_count, 2 * HD)
-    )
-    d_query_low = (
-        rotate(d_queries.transpose(1, 0, 2), own_pos, -1.0)
-        .astype(BF16)
-        .reshape(row_count, head_count * HD)
-    )
+        jnp.concatenate([turn(d_kv_own[:HD], cosine, -sine), d_kv_own[HD:]], axis=0).T
+    ).astype(BF16)
 
     tokens_grads = []
     for h in halves:
@@ -446,45 +747,40 @@
         tokens_grads.append(here.gather_tp(own_grad, z_first[h], ztable))
     tokens_grad = jnp.concatenate(tokens_grads)
 
-    grad_attn = here.scatter_weights(
-        jnp.concatenate(
-            [
-                outer(normed_one, d_query_low),
-                outer(normed_one, d_kv_low),
-                outer(both(d_branch), mixed),
-            ],
-            axis=1,
-        )
-    )
-    grad_query = grad_attn[:, :q_cols]
-    grad_kv_flat = grad_attn[:, q_cols : q_cols + kv_cols]
-    grad_out = grad_attn[:, q_cols + kv_cols :].T
-
-    low = lambda w: w.astype(BF16).astype(F32)
-    gain_one = jnp.sum(low(query_weight) * grad_query, axis=1) + jnp.sum(
-        low(kv_flat) * grad_kv_flat, axis=1
-    )
-    gain_two = jnp.sum(low(gate_weight) * grad_gate + low(up_weight) * grad_up, axis=1)
-    grad_gains = here.sum_tp(jnp.stack([gain_one, gain_two])) / gains_low.astype(F32)
-    grad_kv = grad_kv_flat.reshape(kv_weight.shape)
-
-    out_fan = max(1, 4 * D // group_rows)
-    query_new = adamw_step(query_weight, query_m, query_v, grad_query, D ** (-0.5), DECAY_RATE)
-    kv_new = adamw_step(kv_weight, kv_m, kv_v, grad_kv, D ** (-0.5), DECAY_RATE)
-    out_new = adamw_step(out_weight, out_m, out_v, grad_out, out_fan ** (-0.5), DECAY_RATE)
-    gate_new = adamw_step(gate_weight, gate_m, gate_v, grad_gate, D ** (-0.5), DECAY_RATE)
-    up_new = adamw_step(up_weight, up_m, up_v, grad_up, D ** (-0.5), DECAY_RATE)
-    down_new = adamw_step(down_weight, down_m, down_v, grad_down, FF ** (-0.5), DECAY_RATE)
+    attn_keep, attn_got = here.scatter_weights(
+        *outer_blocks(
+            order,
+            [((normed_one, d_query_low),), ((normed_one, d_kv_low),)]
+            + pairs(d_branch, mixed_half),
+        )
+    )
+    columns = lambda low, high: (attn_keep[:, low:high], attn_got[:, low:high])
+    flat = lambda v: v.reshape(kv_flat.shape)
+    fan = D ** (-0.5)
+    out_fan = max(1, 4 * D // group_rows) ** (-0.5)
+    query_new = adamw_kernel(query_weight, query_m, query_v, *columns(0, q_cols), fan, False)
+    kv_new = adamw_kernel(
+        kv_flat, flat(kv_m), flat(kv_v), *columns(q_cols, q_cols + kv_cols), fan, False
+    )
+    out_new = adamw_kernel(
+        out_weight, out_m, out_v, *columns(q_cols + kv_cols, cols), out_fan, True
+    )
+    gate_new = adamw_kernel(gate_weight, gate_m, gate_v, *gate_sum, fan, False)
+    up_new = adamw_kernel(up_weight, up_m, up_v, *up_sum, fan, False)
+    down_new = adamw_kernel(down_weight, down_m, down_v, *down_sum, FF ** (-0.5), True)
+
+    gain_sums = jnp.stack([query_new[3] + kv_new[3], gate_new[3] + up_new[3]])[:, :, 0]
+    grad_gains = here.sum_tp(gain_sums) / gains_low.astype(F32)
     gains_new = adamw_step(norm_gains, gains_m, gains_v, grad_gains, 0.5, 0.0)
     return (
         output,
         tokens_grad,
-        *query_new,
-        *kv_new,
-        *out_new,
-        *gate_new,
-        *up_new,
-        *down_new,
+        *query_new[:3],
+        *[v.reshape(kv_weight.shape) for v in kv_new[:3]],
+        *out_new[:3],
+        *gate_new[:3],
+        *up_new[:3],
+        *down_new[:3],
         *gains_new,
     )
 

time: 1700 us -> 621 us (0.37)
  Pallas kernels: 889 us -> 110 us
  matrix products: 161 us -> 27.9 us
  other arithmetic: 139 us -> 39 us
  local copies, waits for them, and re-layouts: 132 us -> 38.4 us
  waiting for transfers between devices: 189 us -> 225 us
    pallas_call x11, Pallas kernels: 889 us -> 43.9 us  [place(): pl.pallas_call(kernel, out_shape=[jax.ShapeDtypeStruct(s, BF16) for s in...]
    dot_general x36 -> x0, matrix products: 126 us -> none  [the longest x4 27.3 us: backward_head(): jnp.einsum('rd,kd->rk', query_head, key_head, preferred_element_type=F32)]
    pallas_call x0 -> x14, Pallas kernels: none -> 66.3 us  [the longest x4 37.8 us: outer_blocks(): pl.pallas_call(kernel, grid_spec=pltpu.PrefetchScalarGridSpec(num_scalar_...]
    convert_element_type x8 -> x6, other arithmetic: 54 us -> 4.24 us  [the longest x4 4.04 us: scatter_weights(): total = total + lax.ppermute(both(k).astype(BF16), 'x', ring(k)).astype(F32)]
    dynamic_slice x7 -> x0, local copies, waits for them, and re-layouts: 28.4 us -> none  [the longest x3 25.4 us: pick(): return lax.dynamic_index_in_dim(blocks, index, axis, keepdims=False)]
    unnamed x350 -> x242, local copies, waits for them, and re-layouts: 50.4 us -> 26.8 us
  transfers between devices with their start and end apart: 121 -> 121, of which waited for: 40 -> 52; matrix products, arithmetic and copies ran while one was open for 19% -> 10% of each run, Pallas kernels for 23% -> 14%
where the time goes in v2:
time: 621 us; the launch traced here: 611 us
  waiting for transfers between devices  225 us (36%)
  starting transfers between devices  166 us (27%)
  Pallas kernels  110 us (18%)
  other arithmetic  39 us (6%)
  local copies, waits for them, and re-layouts  38.4 us (6%)
  matrix products  27.9 us (4%)
    ppermute x6, waiting for transfers between devices, gather_weights(): mine = [pair] + [lax.ppermute(pair, 'x', ring(-k)) for k in (1, 2, 3)]  49.7 us
    pallas_call x11, Pallas kernels, place(): pl.pallas_call(kernel, out_shape=[jax.ShapeDtypeStruct(s, BF16) for s in...  43.9 us
    ppermute x12, waiting for transfers between devices, scatter_weights(): total = total + lax.ppermute(both(k).astype(BF16), 'x', ring(k)).astype(F32)  41 us
    pallas_call x4, Pallas kernels, outer_blocks(): pl.pallas_call(kernel, grid_spec=pltpu.PrefetchScalarGridSpec(num_scalar_...  37.8 us
    ppermute x12, waiting for transfers between devices, scatter_tp(): lax.ppermute(pick(blocks, 1, (self.z + k) % 4), 'z', ring(k))  28.4 us
    unnamed x242, local copies, waits for them, and re-layouts  26.8 us
    ppermute x12, waiting for transfers between devices, gather_tp(): pieces = [pair] + [lax.ppermute(pair, 'z', ring(-k)) for k in (1, 2, 3)]  22.8 us
    ppermute x16, waiting for transfers between devices, gather_tp(): theirs = [lax.ppermute(p, 'yl', SWAP) for p in mine]  21.2 us
  transfers between devices with their start and end apart: 121, of which 52 were waited for; matrix products, arithmetic and copies ran while one was open for 10% of the time, Pallas kernels for 14%

profile of v2, /device:TPU:0, one launch (start us, length us, event | category | flops | bytes accessed | tf_op | source)
XLA Modules:
  0.0 610.5 jit_solution(9536843623200583805)
XLA Ops:
  17.9 12.0 %collective-permute-done.1.refs_1_ = bf16[2,144,640]{2,1,0:T(8,128)(2,1)S(1)} collective-permute-done((bf16[2,144,640]{2,1,0:T(8,128)(2,1)S(1)}, bf16[2,144,640]{2,1,0:T(8,128)(2,1)S(1)}, u32[]{:S(2)}, u32[]{:S(2)}) %collective-permute-start.1) | collective-permute-done | bytes 368672 | tf_op jit(solution)/shard_map/ppermute | solution.py:503
  64.7 4.4 collective-permute-done.8.refs_1_
  78.4 4.8 shard_map.423
  86.9 4.1 collective-permute-start.37
  92.4 14.6 %collective-permute-start.19 = (bf16[3,128,1024]{2,1,0:T(8,128)(2,1)S(1)}, bf16[3,128,1024]{2,1,0:T(8,128)(2,1)S(1)}, u32[]{:S(2)}, u32[]{:S(2)}) collective-permute-start(bf16[3,128,1024]{2,1,0:T(8,128)(2,1)S(1)} %pad_maximum_fusion.3), channel_id=1, source_target_pairs={{0,16},{16,0},{1,17},{17,1},{2,18},{18,2},{3,19},{19,3},{4,20},{20... | collective-permute-start | bytes 2359304 | tf_op jit(solution)/shard_map/ppermute | solution.py:502
  107.0 5.1 collective-permute-done.35
  115.9 12.3 %collective-permute-done.19 = bf16[3,128,1024]{2,1,0:T(8,128)(2,1)S(1)} collective-permute-done((bf16[3,128,1024]{2,1,0:T(8,128)(2,1)S(1)}, bf16[3,128,1024]{2,1,0:T(8,128)(2,1)S(1)}, u32[]{:S(2)}, u32[]{:S(2)}) %collective-permute-start.19) | collective-permute-done | bytes 786464 | tf_op jit(solution)/shard_map/ppermute | solution.py:502
  128.3 7.3 %collective-permute-start.20 = (bf16[2,3,128,1024]{3,2,1,0:T(8,128)(2,1)S(1)}, bf16[2,3,128,1024]{3,2,1,0:T(8,128)(2,1)}, u32[]{:S(2)}, u32[]{:S(2)}) collective-permute-start(bf16[2,3,128,1024]{3,2,1,0:T(8,128)(2,1)S(1)} %pad_maximum_fusion.2.refs_0_), channel_id=1, source_target_pairs={{0,96},{32,0},{64,32},{96,64},{1,97},{33,1},{65,33},{97,65},{2,98}... | collective-permute-start | bytes 4718600 | tf_op jit(solution)/shard_map/ppermute | solution.py:503
  154.0 5.0 collective-permute-done.41.refs_3_
  172.0 31.0 %collective-permute-done.20.refs_1_ = bf16[2,3,128,1024]{3,2,1,0:T(8,128)(2,1)} collective-permute-done((bf16[2,3,128,1024]{3,2,1,0:T(8,128)(2,1)S(1)}, bf16[2,3,128,1024]{3,2,1,0:T(8,128)(2,1)}, u32[]{:S(2)}, u32[]{:S(2)}) %collective-permute-start.20) | collective-permute-done | bytes 1572896 | tf_op jit(solution)/shard_map/ppermute | solution.py:503
  208.5 4.0 collective-permute-start.16
  213.2 8.2 %collective-permute-done.16.refs_1_ = bf16[2,48,2048]{2,1,0:T(8,128)(2,1)} collective-permute-done((bf16[2,48,2048]{2,1,0:T(8,128)(2,1)S(1)}, bf16[2,48,2048]{2,1,0:T(8,128)(2,1)}, u32[]{:S(2)}, u32[]{:S(2)}) %collective-permute-start.16) | collective-permute-done | bytes 393248 | tf_op jit(solution)/shard_map/ppermute | solution.py:471
  227.9 5.6 collective-permute-done.17.refs_2_
  239.8 4.8 shard_map.424
  249.6 5.5 shard_map.421
  286.4 9.6 %shard_map.435 = (bf16[1024,1024]{1,0:T(8,128)(2,1)S(1)}, bf16[1024,1024]{1,0:T(8,128)(2,1)S(1)}) custom-call(s32[16]{0:T(128)S(1)} %concatenate.67.table_ref, bf16[384,2048]{1,0:T(8,128)(2,1)S(1)} %bitcast.464, bf16[384,2048]{1,0:T(8,128)(2,1)S(1)} %bitcast.460, bf16[384,1024]{1,0:T(8,128)(2,1)S(1)} %get-tuple-element.278.refs_2_, ...), custom_call_target="tpu_custom_call" | custom-call | flops 3221225472 | bytes 4194304 | tf_op jit(solution)/shard_map/pallas_call | solution.py:396
  300.2 4.9 collective-permute-done.48
  309.7 4.9 collective-permute-done.46
  340.5 9.6 %shard_map.437 = (bf16[1024,1024]{1,0:T(8,128)(2,1)S(1)}, bf16[1024,1024]{1,0:T(8,128)(2,1)S(1)}) custom-call(s32[16]{0:T(128)S(1)} %concatenate.67.table_ref, bf16[384,2048]{1,0:T(8,128)(2,1)S(1)} %bitcast.465, bf16[384,2048]{1,0:T(8,128)(2,1)S(1)} %bitcast.461, bf16[384,1024]{1,0:T(8,128)(2,1)S(1)} %get-tuple-element.279.refs_2_, ...), custom_call_target="tpu_custom_call" | custom-call | flops 3221225472 | bytes 4194304 | tf_op jit(solution)/shard_map/pallas_call | solution.py:396
  355.0 8.3 %collective-permute-done.31 = bf16[48,2048]{1,0:T(8,128)(2,1)S(1)} collective-permute-done((bf16[48,2048]{1,0:T(8,128)(2,1)S(1)}, bf16[48,2048]{1,0:T(8,128)(2,1)S(1)}, u32[]{:S(2)}, u32[]{:S(2)}) %collective-permute-start.31) | collective-permute-done | bytes 196640 | tf_op jit(solution)/shard_map/ppermute | solution.py:470
  369.4 9.6 %shard_map.439 = (bf16[1024,1024]{1,0:T(8,128)(2,1)S(1)}, bf16[1024,1024]{1,0:T(8,128)(2,1)S(1)}) custom-call(s32[16]{0:T(128)S(1)} %concatenate.67.table_ref, bf16[384,2048]{1,0:T(8,128)(2,1)S(1)} %copy-done.10, bf16[384,2048]{1,0:T(8,128)(2,1)S(1)} %copy-done.9, bf16[384,1024]{1,0:T(8,128)(2,1)S(1)} %get-tuple-element.280.refs_2_, ...), custom_call_target="tpu_custom_call" | custom-call | flops 3221225472 | bytes 4194304 | tf_op jit(solution)/shard_map/pallas_call | solution.py:396
  381.3 4.8 shard_map.427
  412.4 9.2 %shard_map.428 = (bf16[768,256]{1,0:T(8,128)(2,1)S(1)}, f32[3072,128]{1,0:T(8,128)S(1)}) custom-call(s32[24]{0:T(128)S(1)} %copy-done.80, bf16[768,256]{1,0:T(8,128)(2,1)S(1)} %pad_maximum_fusion.8.d_ref, bf16[3072,128]{1,0:T(8,128)(2,1)S(1)} %bitcast.474, bf16[6,64,512]{2,1,0:T(8,128)(2,1)S(1)} %pad_maximum_fusion.9.qt_ref, ...), custom_call_target="tpu_custom_call" | custom-call | flops 2415919104 | bytes 2097152 | tf_op jit(solution)/shard_map/pallas_call | solution.py:241
  427.0 4.8 shard_map.425
  439.0 8.9 %collective-permute-start.77 = (bf16[768,128]{1,0:T(8,128)(2,1)S(1)}, bf16[768,128]{1,0:T(8,128)(2,1)S(1)}, u32[]{:S(2)}, u32[]{:S(2)}) collective-permute-start(bf16[768,128]{1,0:T(8,128)(2,1)S(1)} %fusion.53), channel_id=1, source_target_pairs={{0,16},{16,0},{1,17},{17,1},{2,18},{18,2},{3,19},{19,3},{4,20},{20... | collective-permute-start | bytes 589832 | tf_op jit(solution)/shard_map/ppermute | solution.py:537
  461.1 10.2 %collective-permute-done.88 = bf16[2,48,2048]{2,1,0:T(8,128)(2,1)S(1)} collective-permute-done((bf16[2,48,2048]{2,1,0:T(8,128)(2,1)S(1)}, bf16[2,48,2048]{2,1,0:T(8,128)(2,1)S(1)}, u32[]{:S(2)}, u32[]{:S(2)}) %collective-permute-start.88) | collective-permute-done | bytes 393248 | tf_op jit(solution)/shard_map/ppermute | solution.py:485
  471.3 8.9 %shard_map.431 = (bf16[1024,640]{1,0:T(8,128)(2,1)S(1)}, bf16[1024,640]{1,0:T(8,128)(2,1)S(1)}) custom-call(s32[16]{0:T(128)S(1)} %concatenate.67.table_ref, bf16[768,2048]{1,0:T(8,128)(2,1)S(1)} %copy-done.82, bf16[384,2048]{1,0:T(8,128)(2,1)S(1)} %bitcast.469, bf16[384,2048]{1,0:T(8,128)(2,1)S(1)} %bitcast.467, ...), custom_call_target="tpu_custom_call" | custom-call | flops 2013265920 | bytes 4194304 | tf_op jit(solution)/shard_map/pallas_call | solution.py:396
  491.3 15.7 %collective-permute-done.110 = bf16[256,1024]{1,0:T(8,128)(2,1)S(1)} collective-permute-done((bf16[256,1024]{1,0:T(8,128)(2,1)S(1)}, bf16[256,1024]{1,0:T(8,128)(2,1)S(1)}, u32[]{:S(2)}, u32[]{:S(2)}) %collective-permute-start.110) | collective-permute-done | bytes 524320 | tf_op jit(solution)/shard_map/ppermute | solution.py:512
  516.3 10.6 %collective-permute-done.115 = bf16[256,1024]{1,0:T(8,128)(2,1)S(1)} collective-permute-done((bf16[256,1024]{1,0:T(8,128)(2,1)S(1)}, bf16[256,1024]{1,0:T(8,128)(2,1)S(1)}, u32[]{:S(2)}, u32[]{:S(2)}) %collective-permute-start.115) | collective-permute-done | bytes 524320 | tf_op jit(solution)/shard_map/ppermute | solution.py:512
  554.8 6.0 collective-permute-done.100
  563.3 5.2 collective-permute-done.98
  592.3 4.8 shard_map.430
  (618 shorter events, 342.6 us)
Async XLA Ops:
  84.0 28.8 %collective-permute-start.11 = (bf16[4,48,2048]{2,1,0:T(8,128)(2,1)S(1)}, bf16[4,48,2048]{2,1,0:T(8,128)(2,1)S(1)}, u32[]{:S(2)}, u32[]{:S(2)}) collective-permute-start(bf16[4,48,2048]{2,1,0:T(8,128)(2,1)S(1)} %dynamic-slice_bitcast_fusion.3), channel_id=1, source_target_pairs={{0,4},{4,0},{1,5},{5,1},{2,6},{6,2},{3,7},{7,3},{8,12},{12,8},{9,1... | collective-permute-start | bytes 2359304 | tf_op jit(solution)/shard_map/ppermute | solution.py:493
  92.4 35.8 %collective-permute-start.19 = (bf16[3,128,1024]{2,1,0:T(8,128)(2,1)S(1)}, bf16[3,128,1024]{2,1,0:T(8,128)(2,1)S(1)}, u32[]{:S(2)}, u32[]{:S(2)}) collective-permute-start(bf16[3,128,1024]{2,1,0:T(8,128)(2,1)S(1)} %pad_maximum_fusion.3), channel_id=1, source_target_pairs={{0,16},{16,0},{1,17},{17,1},{2,18},{18,2},{3,19},{19,3},{4,20},{20... | collective-permute-start | bytes 2359304 | tf_op jit(solution)/shard_map/ppermute | solution.py:502
  112.3 23.3 %collective-permute-start.38 = (bf16[48,2048]{1,0:T(8,128)(2,1)S(1)}, bf16[48,2048]{1,0:T(8,128)(2,1)S(1)}, u32[]{:S(2)}, u32[]{:S(2)}) collective-permute-start(bf16[48,2048]{1,0:T(8,128)(2,1)S(1)} %fusion.37), channel_id=1, source_target_pairs={{0,4},{4,0},{1,5},{5,1},{2,6},{6,2},{3,7},{7,3},{8,12},{12,8},{9,1... | collective-permute-start | bytes 589832 | tf_op jit(solution)/shard_map/ppermute | solution.py:492
  113.2 22.4 %collective-permute-start.14 = (bf16[48,2048]{1,0:T(8,128)(2,1)S(1)}, bf16[48,2048]{1,0:T(8,128)(2,1)S(1)}, u32[]{:S(2)}, u32[]{:S(2)}) collective-permute-start(bf16[48,2048]{1,0:T(8,128)(2,1)S(1)} %get-tuple-element.306), channel_id=1, source_target_pairs={{0,3},{1,0},{2,1},{3,2},{4,7},{5,4},{6,5},{7,6},{8,11},{9,8},{10,9... | collective-permute-start | bytes 589832 | tf_op jit(solution)/shard_map/ppermute | solution.py:498
  113.2 23.3 %collective-permute-start.13 = (bf16[48,2048]{1,0:T(8,128)(2,1)S(1)}, bf16[48,2048]{1,0:T(8,128)(2,1)S(1)}, u32[]{:S(2)}, u32[]{:S(2)}) collective-permute-start(bf16[48,2048]{1,0:T(8,128)(2,1)S(1)} %get-tuple-element.307), channel_id=1, source_target_pairs={{0,2},{1,3},{2,0},{3,1},{4,6},{5,7},{6,4},{7,5},{8,10},{9,11},{10,... | collective-permute-start | bytes 589832 | tf_op jit(solution)/shard_map/ppermute | solution.py:498
  113.4 23.2 %collective-permute-start.12 = (bf16[48,2048]{1,0:T(8,128)(2,1)S(1)}, bf16[48,2048]{1,0:T(8,128)(2,1)S(1)}, u32[]{:S(2)}, u32[]{:S(2)}) collective-permute-start(bf16[48,2048]{1,0:T(8,128)(2,1)S(1)} %get-tuple-element.305), channel_id=1, source_target_pairs={{0,1},{1,2},{2,3},{3,0},{4,5},{5,6},{6,7},{7,4},{8,9},{9,10},{10,1... | collective-permute-start | bytes 589832 | tf_op jit(solution)/shard_map/ppermute | solution.py:498
  128.3 74.7 %collective-permute-start.20 = (bf16[2,3,128,1024]{3,2,1,0:T(8,128)(2,1)S(1)}, bf16[2,3,128,1024]{3,2,1,0:T(8,128)(2,1)}, u32[]{:S(2)}, u32[]{:S(2)}) collective-permute-start(bf16[2,3,128,1024]{3,2,1,0:T(8,128)(2,1)S(1)} %pad_maximum_fusion.2.refs_0_), channel_id=1, source_target_pairs={{0,96},{32,0},{64,32},{96,64},{1,97},{33,1},{65,33},{97,65},{2,98}... | collective-permute-start | bytes 4718600 | tf_op jit(solution)/shard_map/ppermute | solution.py:503
  135.6 68.6 %collective-permute-start.21 = (bf16[2,3,128,1024]{3,2,1,0:T(8,128)(2,1)S(1)}, bf16[2,3,128,1024]{3,2,1,0:T(8,128)(2,1)}, u32[]{:S(2)}, u32[]{:S(2)}) collective-permute-start(bf16[2,3,128,1024]{3,2,1,0:T(8,128)(2,1)S(1)} %pad_maximum_fusion.2.refs_0_), channel_id=1, source_target_pairs={{0,64},{32,96},{64,0},{96,32},{1,65},{33,97},{65,1},{97,33},{2,66}... | collective-permute-start | bytes 4718600 | tf_op jit(solution)/shard_map/ppermute | solution.py:503
  135.6 72.0 %collective-permute-start.22 = (bf16[2,3,128,1024]{3,2,1,0:T(8,128)(2,1)S(1)}, bf16[2,3,128,1024]{3,2,1,0:T(8,128)(2,1)}, u32[]{:S(2)}, u32[]{:S(2)}) collective-permute-start(bf16[2,3,128,1024]{3,2,1,0:T(8,128)(2,1)S(1)} %pad_maximum_fusion.2.refs_0_), channel_id=1, source_target_pairs={{0,32},{32,64},{64,96},{96,0},{1,33},{33,65},{65,97},{97,1},{2,34}... | collective-permute-start | bytes 4718600 | tf_op jit(solution)/shard_map/ppermute | solution.py:503
  167.4 82.2 %collective-permute-start.23 = (bf16[2,3,128,1024]{3,2,1,0:T(8,128)(2,1)S(1)}, bf16[2,3,128,1024]{3,2,1,0:T(8,128)(2,1)}, u32[]{:S(2)}, u32[]{:S(2)}) collective-permute-start(bf16[2,3,128,1024]{3,2,1,0:T(8,128)(2,1)S(1)} %pad_maximum_fusion.2.refs_0_), channel_id=1, source_target_pairs={{0,8},{8,0},{1,9},{9,1},{2,10},{10,2},{3,11},{11,3},{4,12},{12,4},... | collective-permute-start | bytes 4718600 | tf_op jit(solution)/shard_map/ppermute | solution.py:504
  171.0 36.8 %collective-permute-start.45 = (bf16[48,2048]{1,0:T(8,128)(2,1)S(1)}, bf16[48,2048]{1,0:T(8,128)(2,1)S(1)}, u32[]{:S(2)}, u32[]{:S(2)}) collective-permute-start(bf16[48,2048]{1,0:T(8,128)(2,1)S(1)} %collective-permute-done.41.refs_3_), channel_id=1, source_target_pairs={{0,4},{4,0},{1,5},{5,1},{2,6},{6,2},{3,7},{7,3},{8,12},{12,8},{9,1... | collective-permute-start | bytes 589832 | tf_op jit(solution)/shard_map/ppermute | solution.py:475
  203.0 46.6 %collective-permute-start.24 = (bf16[2,3,128,1024]{3,2,1,0:T(8,128)(2,1)}, bf16[2,3,128,1024]{3,2,1,0:T(8,128)(2,1)}, u32[]{:S(2)}, u32[]{:S(2)}) collective-permute-start(bf16[2,3,128,1024]{3,2,1,0:T(8,128)(2,1)} %collective-permute-done.20.refs_1_), channel_id=1, source_target_pairs={{0,8},{8,0},{1,9},{9,1},{2,10},{10,2},{3,11},{11,3},{4,12},{12,4},... | collective-permute-start | bytes 4718600 | tf_op jit(solution)/shard_map/ppermute | solution.py:504
  204.2 45.4 %collective-permute-start.25 = (bf16[2,3,128,1024]{3,2,1,0:T(8,128)(2,1)}, bf16[2,3,128,1024]{3,2,1,0:T(8,128)(2,1)}, u32[]{:S(2)}, u32[]{:S(2)}) collective-permute-start(bf16[2,3,128,1024]{3,2,1,0:T(8,128)(2,1)} %collective-permute-done.21.refs_2_), channel_id=1, source_target_pairs={{0,8},{8,0},{1,9},{9,1},{2,10},{10,2},{3,11},{11,3},{4,12},{12,4},... | collective-permute-start | bytes 4718600 | tf_op jit(solution)/shard_map/ppermute | solution.py:504
  207.6 42.0 %collective-permute-start.26 = (bf16[2,3,128,1024]{3,2,1,0:T(8,128)(2,1)}, bf16[2,3,128,1024]{3,2,1,0:T(8,128)(2,1)}, u32[]{:S(2)}, u32[]{:S(2)}) collective-permute-start(bf16[2,3,128,1024]{3,2,1,0:T(8,128)(2,1)} %collective-permute-done.22.refs_3_), channel_id=1, source_target_pairs={{0,8},{8,0},{1,9},{9,1},{2,10},{10,2},{3,11},{11,3},{4,12},{12,4},... | collective-permute-start | bytes 4718600 | tf_op jit(solution)/shard_map/ppermute | solution.py:504
  266.9 49.8 %collective-permute-start.57 = (bf16[4,48,2048]{2,1,0:T(8,128)(2,1)S(1)}, bf16[4,48,2048]{2,1,0:T(8,128)(2,1)}, u32[]{:S(2)}, u32[]{:S(2)}) collective-permute-start(bf16[4,48,2048]{2,1,0:T(8,128)(2,1)S(1)} %dynamic-slice_bitcast_fusion.1), channel_id=1, source_target_pairs={{0,4},{4,0},{1,5},{5,1},{2,6},{6,2},{3,7},{7,3},{8,12},{12,8},{9,1... | collective-permute-start | bytes 2359304 | tf_op jit(solution)/shard_map/ppermute | solution.py:493
  282.7 22.5 %collective-permute-start.48 = (bf16[2,48,2048]{2,1,0:T(8,128)(2,1)}, bf16[2,48,2048]{2,1,0:T(8,128)(2,1)}, u32[]{:S(2)}, u32[]{:S(2)}) collective-permute-start(bf16[2,48,2048]{2,1,0:T(8,128)(2,1)} %get-tuple-element.291), channel_id=1, source_target_pairs={{0,3},{1,0},{2,1},{3,2},{4,7},{5,4},{6,5},{7,6},{8,11},{9,8},{10,9... | collective-permute-start | bytes 1179656 | tf_op jit(solution)/shard_map/ppermute | solution.py:485
  363.2 24.7 %collective-permute-start.62 = (bf16[2,48,2048]{2,1,0:T(8,128)(2,1)S(1)}, bf16[2,48,2048]{2,1,0:T(8,128)(2,1)S(1)}, u32[]{:S(2)}, u32[]{:S(2)}) collective-permute-start(bf16[2,48,2048]{2,1,0:T(8,128)(2,1)S(1)} %pad_maximum_fusion.7.refs_0_), channel_id=1, source_target_pairs={{0,3},{1,0},{2,1},{3,2},{4,7},{5,4},{6,5},{7,6},{8,11},{9,8},{10,9... | collective-permute-start | bytes 1179656 | tf_op jit(solution)/shard_map/ppermute | solution.py:471
  365.3 24.1 %collective-permute-start.63 = (bf16[2,48,2048]{2,1,0:T(8,128)(2,1)S(1)}, bf16[2,48,2048]{2,1,0:T(8,128)(2,1)S(1)}, u32[]{:S(2)}, u32[]{:S(2)}) collective-permute-start(bf16[2,48,2048]{2,1,0:T(8,128)(2,1)S(1)} %pad_maximum_fusion.7.refs_0_), channel_id=1, source_target_pairs={{0,2},{1,3},{2,0},{3,1},{4,6},{5,7},{6,4},{7,5},{8,10},{9,11},{10,... | collective-permute-start | bytes 1179656 | tf_op jit(solution)/shard_map/ppermute | solution.py:471
  367.3 22.5 %collective-permute-start.64 = (bf16[2,48,2048]{2,1,0:T(8,128)(2,1)S(1)}, bf16[2,48,2048]{2,1,0:T(8,128)(2,1)S(1)}, u32[]{:S(2)}, u32[]{:S(2)}) collective-permute-start(bf16[2,48,2048]{2,1,0:T(8,128)(2,1)S(1)} %pad_maximum_fusion.7.refs_0_), channel_id=1, source_target_pairs={{0,1},{1,2},{2,3},{3,0},{4,5},{5,6},{6,7},{7,4},{8,9},{9,10},{10,1... | collective-permute-start | bytes 1179656 | tf_op jit(solution)/shard_map/ppermute | solution.py:471
  379.0 68.9 %collective-permute-start.102 = (bf16[1024,1024]{1,0:T(8,128)(2,1)S(1)}, bf16[1024,1024]{1,0:T(8,128)(2,1)S(1)}, u32[]{:S(2)}, u32[]{:S(2)}) collective-permute-start(bf16[1024,1024]{1,0:T(8,128)(2,1)S(1)} %get-tuple-element.119), channel_id=1, source_target_pairs={{0,8},{8,0},{1,9},{9,1},{2,10},{10,2},{3,11},{11,3},{4,12},{12,4},... | collective-permute-start | bytes 6291464 | tf_op jit(solution)/shard_map/ppermute | solution.py:507
  387.9 64.3 %collective-permute-start.107 = (bf16[1024,1024]{1,0:T(8,128)(2,1)S(1)}, bf16[1024,1024]{1,0:T(8,128)(2,1)S(1)}, u32[]{:S(2)}, u32[]{:S(2)}) collective-permute-start(bf16[1024,1024]{1,0:T(8,128)(2,1)S(1)} %get-tuple-element.124), channel_id=1, source_target_pairs={{0,8},{8,0},{1,9},{9,1},{2,10},{10,2},{3,11},{11,3},{4,12},{12,4},... | collective-permute-start | bytes 6291464 | tf_op jit(solution)/shard_map/ppermute | solution.py:507
  396.7 58.0 %collective-permute-start.112 = (bf16[1024,1024]{1,0:T(8,128)(2,1)S(1)}, bf16[1024,1024]{1,0:T(8,128)(2,1)S(1)}, u32[]{:S(2)}, u32[]{:S(2)}) collective-permute-start(bf16[1024,1024]{1,0:T(8,128)(2,1)S(1)} %get-tuple-element.129), channel_id=1, source_target_pairs={{0,8},{8,0},{1,9},{9,1},{2,10},{10,2},{3,11},{11,3},{4,12},{12,4},... | collective-permute-start | bytes 6291464 | tf_op jit(solution)/shard_map/ppermute | solution.py:507
  449.5 36.5 %collective-permute-start.105 = (bf16[256,1024]{1,0:T(8,128)(2,1)}, bf16[256,1024]{1,0:T(8,128)(2,1)}, u32[]{:S(2)}, u32[]{:S(2)}) collective-permute-start(bf16[256,1024]{1,0:T(8,128)(2,1)} %get-tuple-element.267), channel_id=1, source_target_pairs={{0,96},{32,0},{64,32},{96,64},{1,97},{33,1},{65,33},{97,65},{2,98}... | collective-permute-start | bytes 1572872 | tf_op jit(solution)/shard_map/ppermute | solution.py:512
  452.2 33.8 %collective-permute-start.104 = (bf16[256,1024]{1,0:T(8,128)(2,1)}, bf16[256,1024]{1,0:T(8,128)(2,1)}, u32[]{:S(2)}, u32[]{:S(2)}) collective-permute-start(bf16[256,1024]{1,0:T(8,128)(2,1)} %get-tuple-element.268), channel_id=1, source_target_pairs={{0,64},{32,96},{64,0},{96,32},{1,65},{33,97},{65,1},{97,33},{2,66}... | collective-permute-start | bytes 1572872 | tf_op jit(solution)/shard_map/ppermute | solution.py:512
  452.2 34.5 %collective-permute-start.103 = (bf16[256,1024]{1,0:T(8,128)(2,1)}, bf16[256,1024]{1,0:T(8,128)(2,1)}, u32[]{:S(2)}, u32[]{:S(2)}) collective-permute-start(bf16[256,1024]{1,0:T(8,128)(2,1)} %get-tuple-element.266), channel_id=1, source_target_pairs={{0,32},{32,64},{64,96},{96,0},{1,33},{33,65},{65,97},{97,1},{2,34}... | collective-permute-start | bytes 1572872 | tf_op jit(solution)/shard_map/ppermute | solution.py:512
  481.3 25.7 %collective-permute-start.110 = (bf16[256,1024]{1,0:T(8,128)(2,1)S(1)}, bf16[256,1024]{1,0:T(8,128)(2,1)S(1)}, u32[]{:S(2)}, u32[]{:S(2)}) collective-permute-start(bf16[256,1024]{1,0:T(8,128)(2,1)S(1)} %copy-done.97), channel_id=1, source_target_pairs={{0,96},{32,0},{64,32},{96,64},{1,97},{33,1},{65,33},{97,65},{2,98}... | collective-permute-start | bytes 1572872 | tf_op jit(solution)/shard_map/ppermute | solution.py:512
  483.7 25.7 %collective-permute-start.109 = (bf16[256,1024]{1,0:T(8,128)(2,1)S(1)}, bf16[256,1024]{1,0:T(8,128)(2,1)S(1)}, u32[]{:S(2)}, u32[]{:S(2)}) collective-permute-start(bf16[256,1024]{1,0:T(8,128)(2,1)S(1)} %copy-done.96), channel_id=1, source_target_pairs={{0,64},{32,96},{64,0},{96,32},{1,65},{33,97},{65,1},{97,33},{2,66}... | collective-permute-start | bytes 1572872 | tf_op jit(solution)/shard_map/ppermute | solution.py:512
  486.0 25.8 %collective-permute-start.108 = (bf16[256,1024]{1,0:T(8,128)(2,1)S(1)}, bf16[256,1024]{1,0:T(8,128)(2,1)S(1)}, u32[]{:S(2)}, u32[]{:S(2)}) collective-permute-start(bf16[256,1024]{1,0:T(8,128)(2,1)S(1)} %copy-done.95), channel_id=1, source_target_pairs={{0,32},{32,64},{64,96},{96,0},{1,33},{33,65},{65,97},{97,1},{2,34}... | collective-permute-start | bytes 1572872 | tf_op jit(solution)/shard_map/ppermute | solution.py:512
  486.0 27.7 %collective-permute-start.78 = (bf16[4,48,2048]{2,1,0:T(8,128)(2,1)S(1)}, bf16[4,48,2048]{2,1,0:T(8,128)(2,1)S(1)}, u32[]{:S(2)}, u32[]{:S(2)}) collective-permute-start(bf16[4,48,2048]{2,1,0:T(8,128)(2,1)S(1)} %dynamic-slice_bitcast_fusion), channel_id=1, source_target_pairs={{0,4},{4,0},{1,5},{5,1},{2,6},{6,2},{3,7},{7,3},{8,12},{12,8},{9,1... | collective-permute-start | bytes 2359304 | tf_op jit(solution)/shard_map/ppermute | solution.py:493
  486.8 40.1 %collective-permute-start.115 = (bf16[256,1024]{1,0:T(8,128)(2,1)S(1)}, bf16[256,1024]{1,0:T(8,128)(2,1)S(1)}, u32[]{:S(2)}, u32[]{:S(2)}) collective-permute-start(bf16[256,1024]{1,0:T(8,128)(2,1)S(1)} %get-tuple-element.261), channel_id=1, source_target_pairs={{0,96},{32,0},{64,32},{96,64},{1,97},{33,1},{65,33},{97,65},{2,98}... | collective-permute-start | bytes 1572872 | tf_op jit(solution)/shard_map/ppermute | solution.py:512
  526.9 22.9 %collective-permute-start.97 = (bf16[1024,640]{1,0:T(8,128)(2,1)S(1)}, bf16[1024,640]{1,0:T(8,128)(2,1)S(1)}, u32[]{:S(2)}, u32[]{:S(2)}) collective-permute-start(bf16[1024,640]{1,0:T(8,128)(2,1)S(1)} %get-tuple-element.108), channel_id=1, source_target_pairs={{0,8},{8,0},{1,9},{9,1},{2,10},{10,2},{3,11},{11,3},{4,12},{12,4},... | collective-permute-start | bytes 3932168 | tf_op jit(solution)/shard_map/ppermute | solution.py:507
  539.2 41.4 %collective-permute-start.116 = (bf16[128,1024]{1,0:T(8,128)(2,1)S(1)}, bf16[128,1024]{1,0:T(8,128)(2,1)S(1)}, u32[]{:S(2)}, u32[]{:S(2)}) collective-permute-start(bf16[128,1024]{1,0:T(8,128)(2,1)S(1)} %slice.380), channel_id=1, source_target_pairs={{0,16},{16,0},{1,17},{17,1},{2,18},{18,2},{3,19},{19,3},{4,20},{20... | collective-permute-start | bytes 786440 | tf_op jit(solution)/shard_map/ppermute | solution.py:513
  (209 other events, 2374.3 us)
